TPU v7x, 512 devices: a whole 4x8x8 slice. The times are simulated.
512 devices in a mesh: band: 4 (over x_hi, core), dom: 128 (over x_lo, z, y).
Axes of the slice: x: 4 (x_hi: 2, x_lo: 2; x = x_hi * 2 + x_lo), y: 8, z: 8, core: 2. Of those that a mesh axis runs over, the one named last changes fastest.
Arguments:
- states: float32 [128, 524288], P('band', 'dom'), may hold values from -6 to 6
- previous: float32 [128, 524288], P('band', 'dom'), may hold values from -6 to 6
- potential: float32 [524288], P('dom'), may hold values from -2 to 2
- tile_atom: int32 [8192], P('dom'), may hold values from 0 to 511, as said below
- tile_cells: int32 [8192, 128], P('dom'), may hold values from 0 to 4095
- tile_count: int32 [128], P('dom'), may hold values from 8 to 64, as said below
- projectors: float32 [8192, 8, 128], P('dom'), may hold values from -3 to 3
- coupling: float32 [512, 8, 8], P('dom'), may hold values from -2 to 2
- rotation: float32 [128, 128], replicated, may hold values from -0.5 to 0.5
Outputs:
- rotated: float32 [524288, 128], P(('dom', 'band'))
Inputs may be any that keep to these rules, and one draw needn't show every extreme that they name: `tile_atom`: atom a belongs to domain a // 4; the atom of a tile belongs to the tile's own domain or to a domain sharing a face with it. Tiles 0 to tile_count - 1 of a domain are live, the others carry nothing. `tile_cells`: cells of the tile's own domain; a cell may repeat.
All inputs are finite; a program needn't handle non-finite values.
Results may differ from a plain program's by a relative error of at most 0.000071.
Values sent between devices are 32-bit elements; how exact they have to be, the bound alone decides.
A program may use at most 64 MiB of HBM per device.

v0:
```python
import jax
import jax.numpy as jnp
from jax import lax
from jax.sharding import PartitionSpec as P

CX = 8
CY = 8
CZ = 64


stencil_weights = (
    -5369.0 / 1800.0,
    12.0 / 7.0,
    -15.0 / 56.0,
    10.0 / 189.0,
    -1.0 / 112.0,
    2.0 / 1925.0,
    -1.0 / 16632.0,
)


def shifted(block, axis, distance):
    devices = range(lax.axis_size(axis))
    route = [(i - distance, i) for i in devices if i - distance in devices]
    return lax.ppermute(block, axis, route)


def neighbour(piece, offset, wanted):
    moved = shifted(piece, "dom", offset)
    return jnp.where(wanted, moved, jnp.zeros_like(moved))


def pass_sums(piece, offset, wanted):
    moved = shifted(piece, "dom", offset)
    return jnp.where(wanted, moved, jnp.zeros_like(moved))


def pass_coefs(piece, offset, wanted):
    moved = shifted(piece, "dom", offset)
    return jnp.where(wanted, moved, jnp.zeros_like(moved))


def body(
    states, previous, potential, tile_atom, tile_cells, tile_count, projectors, coupling, rotation
):
    highest = lax.Precision.HIGHEST
    blocks = states.shape[0]
    cell_count = states.shape[1]
    radius = len(stencil_weights) - 1
    domains = lax.axis_size("dom")
    side_z = min(4, max(2, domains // 32))
    layer_size = side_z * side_z
    my_domain = lax.axis_index("dom")
    z_index = my_domain % side_z
    y_index = my_domain // side_z % side_z
    x_index = my_domain // layer_size
    x_final = domains // layer_size - 1
    blockgrid = states.reshape(blocks, CX, CY, CZ)
    laplace = 3.0 * stencil_weights[0] * blockgrid
    layouts = (
        (1, layer_size, x_index, x_final),
        (2, side_z, y_index, side_z - 1),
        (3, 1, z_index, side_z - 1),
    )
    for dimension, stride, position, final_index in layouts:
        length = blockgrid.shape[dimension]
        below_rim = neighbour(
            lax.slice_in_dim(blockgrid, length - radius, length, axis=dimension),
            stride,
            position > 0,
        )
        above_rim = neighbour(
            lax.slice_in_dim(blockgrid, 0, radius, axis=dimension), -stride, position < final_index
        )
        extended = jnp.concatenate([below_rim, blockgrid, above_rim], axis=dimension)
        for offset in range(1, radius + 1):
            higher = lax.slice_in_dim(
                extended, radius + offset, radius + offset + length, axis=dimension
            )
            lower_side = lax.slice_in_dim(
                extended, radius - offset, radius - offset + length, axis=dimension
            )
            laplace = laplace + stencil_weights[offset] * (higher + lower_side)
    kinetic = (-0.5 * laplace).reshape(blocks, cell_count)
    slots = tile_atom.shape[0]
    atom_here = coupling.shape[0]
    alive = (jnp.arange(slots, dtype=jnp.int32) < tile_count[0]).astype(jnp.float32)
    weights = projectors * alive[:, None, None]
    picked = states[:, tile_cells]
    partial_value = jnp.einsum("stp,tjp->tjs", picked, weights, precision=highest)
    directions = (
        (layer_size, x_index < x_final, x_index > 0),
        (-layer_size, x_index > 0, x_index < x_final),
        (side_z, y_index < side_z - 1, y_index > 0),
        (-side_z, y_index > 0, y_index < side_z - 1),
        (1, z_index < side_z - 1, z_index > 0),
        (-1, z_index > 0, z_index < side_z - 1),
    )
    local_ids = jnp.arange(atom_here, dtype=jnp.int32)
    candidates = [my_domain * atom_here + local_ids]
    for offset, exists, opposite in directions:
        candidates.append((my_domain + offset) * atom_here + local_ids)
    candidate_ids = jnp.concatenate(candidates)
    member = (tile_atom[None, :] == candidate_ids[:, None]).astype(jnp.float32)
    sums = jnp.einsum("at,tjs->ajs", member, partial_value, precision=highest)
    owned = sums[0:atom_here]
    for number, (offset, exists, opposite) in enumerate(directions):
        piece = sums[(number + 1) * atom_here : (number + 2) * atom_here]
        owned = owned + pass_sums(piece, offset, opposite)
    local_coef = jnp.einsum("aij,ajs->ais", coupling, owned, precision=highest)
    coef_parts = [local_coef]
    for offset, exists, opposite in directions:
        coef_parts.append(pass_coefs(local_coef, -offset, exists))
    every_coef = jnp.concatenate(coef_parts, axis=0)
    tile_coef = jnp.einsum("at,ajs->tjs", member, every_coef, precision=highest)
    spread = jnp.einsum("tjp,tjs->stp", weights, tile_coef, precision=highest)
    projected = jnp.zeros_like(states).at[:, tile_cells].add(spread)
    filtered = (
        0.15 * (kinetic + potential[None, :] * states + projected - 8.0 * states) - 0.3 * previous
    )
    received = lax.all_to_all(filtered, "band", split_axis=1, concat_axis=0, tiled=True)
    rotated = lax.dot_general(received, rotation, (((0,), (0,)), ((), ())), precision=highest)
    return rotated


def solution(mesh):
    placed = (
        P("band", "dom"),
        P("band", "dom"),
        P("dom"),
        P("dom"),
        P("dom", None),
        P("dom"),
        P("dom", None, None),
        P("dom", None, None),
        P(),
    )
    return jax.shard_map(
        body, mesh=mesh, in_specs=placed, out_specs=P(("dom", "band"), None), check_vma=False
    )
```

profile of v0, /device:TPU:66, one launch (start us, length us, event | category | flops | bytes accessed | tf_op | source)
XLA Modules:
  0.0 321.9 jit_solution(6672227020097711377)
XLA Ops:
  0.0 1.7 copy.100
  1.7 27.7 %gather_fusion = f32[8192,32]{1,0:T(8,128)} fusion(f32[32,4096]{0,1:T(8,128)S(1)} %copy.100, s32[8192]{0:T(1024)S(1)} %broadcast_clamp_fusion), kind=kCustom, calls=%fused_computation | custom fusion | bytes 2129920 | tf_op jit(solution)/shard_map/gather | solution.py:89
  29.4 2.8 copy.102
  33.0 2.5 fusion.78
  35.5 0.1 concatenate.63
  35.6 0.6 copy-done.10
  36.2 1.2 fusion.81
  37.4 4.5 %collective-permute-start.11 = (f32[4,8,32]{2,0,1:T(4,128)S(1)}, f32[4,8,32]{2,0,1:T(4,128)S(1)}, u32[]{:S(2)}, u32[]{:S(2)}) collective-permute-start(f32[4,8,32]{2,0,1:T(4,128)S(1)} %get-tuple-element.12), channel_id=1, source_target_pairs={{1,0},{2,1},{3,2},{4,3},{5,4},{6,5},{7,6},{8,7},{9,8},{10,9},{11,1... | collective-permute-start | bytes 12296 | tf_op jit(solution)/shard_map/ppermute | solution.py:25
  41.9 1.9 collective-permute-start.10
  43.8 6.3 %collective-permute-start.9 = (f32[4,8,32]{2,0,1:T(4,128)S(1)}, f32[4,8,32]{2,0,1:T(4,128)S(1)}, u32[]{:S(2)}, u32[]{:S(2)}) collective-permute-start(f32[4,8,32]{2,0,1:T(4,128)S(1)} %get-tuple-element.14), channel_id=1, source_target_pairs={{4,0},{5,1},{6,2},{7,3},{8,4},{9,5},{10,6},{11,7},{12,8},{13,9},{1... | collective-permute-start | bytes 12296 | tf_op jit(solution)/shard_map/ppermute | solution.py:25
  50.1 3.5 %collective-permute-start.8 = (f32[4,8,32]{2,0,1:T(4,128)S(1)}, f32[4,8,32]{2,0,1:T(4,128)S(1)}, u32[]{:S(2)}, u32[]{:S(2)}) collective-permute-start(f32[4,8,32]{2,0,1:T(4,128)S(1)} %get-tuple-element.15), channel_id=1, source_target_pairs={{0,4},{1,5},{2,6},{3,7},{4,8},{5,9},{6,10},{7,11},{8,12},{9,13},{1... | collective-permute-start | bytes 12296 | tf_op jit(solution)/shard_map/ppermute | solution.py:25
  53.6 10.9 %collective-permute-start.7 = (f32[4,8,32]{2,0,1:T(4,128)S(1)}, f32[4,8,32]{2,0,1:T(4,128)S(1)}, u32[]{:S(2)}, u32[]{:S(2)}) collective-permute-start(f32[4,8,32]{2,0,1:T(4,128)S(1)} %get-tuple-element.16), channel_id=1, source_target_pairs={{16,0},{17,1},{18,2},{19,3},{20,4},{21,5},{22,6},{23,7},{24,8},{25... | collective-permute-start | bytes 12296 | tf_op jit(solution)/shard_map/ppermute | solution.py:25
  64.5 1.5 reshape.17
  66.0 1.7 fusion.104
  67.7 1.6 fusion.103
  69.3 0.0 collective-permute-done.11
  69.3 1.9 collective-permute-start.6
  71.2 1.3 fusion.102
  72.5 2.5 copy.97
  74.9 2.4 copy.95
  77.4 2.4 copy.93
  79.8 1.1 copy.91
  80.8 2.0 collective-permute-start.5
  82.9 6.8 %collective-permute-start.4 = (f32[32,8,8,6]{0,2,3,1:T(8,128)}, f32[32,8,8,6]{0,2,3,1:T(8,128)}, u32[]{:S(2)}, u32[]{:S(2)}) collective-permute-start(f32[32,8,8,6]{0,2,3,1:T(8,128)} %copy.95), channel_id=1, source_target_pairs={{1,0},{2,1},{3,2},{4,3},{5,4},{6,5},{7,6},{8,7},{9,8},{10,9},{11,1... | collective-permute-start | bytes 147464 | tf_op jit(solution)/shard_map/ppermute | solution.py:25
  89.7 7.5 %collective-permute-start.3 = (f32[32,8,6,64]{3,1,2,0:T(8,128)}, f32[32,8,6,64]{3,1,2,0:T(8,128)}, u32[]{:S(2)}, u32[]{:S(2)}) collective-permute-start(f32[32,8,6,64]{3,1,2,0:T(8,128)} %copy.93), channel_id=1, source_target_pairs={{0,4},{1,5},{2,6},{3,7},{4,8},{5,9},{6,10},{7,11},{8,12},{9,13},{1... | collective-permute-start | bytes 1179656 | tf_op jit(solution)/shard_map/ppermute | solution.py:25
  97.2 3.2 collective-permute-start.2
  100.4 0.8 fusion.95
  101.2 0.2 fusion.96
  101.3 6.9 %collective-permute-start.12 = (f32[4,8,32]{2,0,1:T(4,128)S(1)}, f32[4,8,32]{2,0,1:T(4,128)S(1)}, u32[]{:S(2)}, u32[]{:S(2)}) collective-permute-start(f32[4,8,32]{2,0,1:T(4,128)S(1)} %bitcast.40), channel_id=1, source_target_pairs={{16,0},{17,1},{18,2},{19,3},{20,4},{21,5},{22,6},{23,7},{24,8},{25... | collective-permute-start | bytes 12296 | tf_op jit(solution)/shard_map/ppermute | solution.py:25
  108.3 1.4 collective-permute-done.12
  109.7 1.9 collective-permute-start.13
  111.6 7.4 %collective-permute-done.13 = f32[4,8,32]{2,0,1:T(4,128)S(1)} collective-permute-done((f32[4,8,32]{2,0,1:T(4,128)S(1)}, f32[4,8,32]{2,0,1:T(4,128)S(1)}, u32[]{:S(2)}, u32[]{:S(2)}) %collective-permute-start.13) | collective-permute-done | bytes 4128 | tf_op jit(solution)/shard_map/ppermute | solution.py:25
  119.1 7.1 %collective-permute-start.14 = (f32[4,8,32]{2,0,1:T(4,128)S(1)}, f32[4,8,32]{2,0,1:T(4,128)S(1)}, u32[]{:S(2)}, u32[]{:S(2)}) collective-permute-start(f32[4,8,32]{2,0,1:T(4,128)S(1)} %bitcast.42), channel_id=1, source_target_pairs={{4,0},{5,1},{6,2},{7,3},{8,4},{9,5},{10,6},{11,7},{12,8},{13,9},{1... | collective-permute-start | bytes 12296 | tf_op jit(solution)/shard_map/ppermute | solution.py:25
  126.2 43.7 %collective-permute-done.14 = f32[4,8,32]{2,0,1:T(4,128)S(1)} collective-permute-done((f32[4,8,32]{2,0,1:T(4,128)S(1)}, f32[4,8,32]{2,0,1:T(4,128)S(1)}, u32[]{:S(2)}, u32[]{:S(2)}) %collective-permute-start.14) | collective-permute-done | bytes 4128 | tf_op jit(solution)/shard_map/ppermute | solution.py:25
  169.9 1.9 collective-permute-start.15
  171.8 8.5 %collective-permute-done.15 = f32[4,8,32]{2,0,1:T(4,128)S(1)} collective-permute-done((f32[4,8,32]{2,0,1:T(4,128)S(1)}, f32[4,8,32]{2,0,1:T(4,128)S(1)}, u32[]{:S(2)}, u32[]{:S(2)}) %collective-permute-start.15) | collective-permute-done | bytes 4128 | tf_op jit(solution)/shard_map/ppermute | solution.py:25
  180.3 1.9 collective-permute-start.16
  182.2 3.7 %collective-permute-done.16 = f32[4,8,32]{2,0,1:T(4,128)S(1)} collective-permute-done((f32[4,8,32]{2,0,1:T(4,128)S(1)}, f32[4,8,32]{2,0,1:T(4,128)S(1)}, u32[]{:S(2)}, u32[]{:S(2)}) %collective-permute-start.16) | collective-permute-done | bytes 4128 | tf_op jit(solution)/shard_map/ppermute | solution.py:25
  185.9 1.9 collective-permute-start.17
  187.9 5.8 %collective-permute-done.17 = f32[4,8,32]{2,0,1:T(4,128)S(1)} collective-permute-done((f32[4,8,32]{2,0,1:T(4,128)S(1)}, f32[4,8,32]{2,0,1:T(4,128)S(1)}, u32[]{:S(2)}, u32[]{:S(2)}) %collective-permute-start.17) | collective-permute-done | bytes 4128 | tf_op jit(solution)/shard_map/ppermute | solution.py:25
  193.7 1.9 collective-permute-start.1
  195.6 0.1 concatenate.64
  195.7 0.1 copy.106
  195.8 1.6 fusion.89
  197.4 1.1 copy.107
  198.5 9.3 %fusion.83 = f32[64,128,32]{2,1,0:T(8,128)} fusion(f32[64,8,32]{2,1,0:T(8,128)S(1)} %copy.107, f32[64,8,128]{2,1,0:T(8,128)} %param.15, f32[64]{0:T(128)} %copy-done.12), kind=kOutput, calls=%fused_computation.152 | convolution fusion | flops 25231360 | bytes 1376512 | tf_op jit(solution)/shard_map/tjp,tjs->stp/transpose | solution.py:116
  207.8 8.0 %collective-permute-start = (f32[32,6,8,64]{3,2,1,0:T(8,128)}, f32[32,6,8,64]{3,2,1,0:T(8,128)}, u32[]{:S(2)}, u32[]{:S(2)}) collective-permute-start(f32[32,6,8,64]{3,2,1,0:T(8,128)} %get-tuple-element.5), channel_id=1, source_target_pairs={{16,0},{17,1},{18,2},{19,3},{20,4},{21,5},{22,6},{23,7},{24,8},{25... | collective-permute-start | bytes 1179656 | tf_op jit(solution)/shard_map/ppermute | solution.py:25
  215.8 1.6 broadcast_select_fusion.3
  217.4 1.9 copy.98
  219.3 2.8 copy.96
  222.1 1.4 copy_select_fusion
  223.5 5.1 %collective-permute-done.1 = f32[32,6,8,64]{3,2,1,0:T(8,128)} collective-permute-done((f32[32,6,8,64]{3,2,1,0:T(8,128)}, f32[32,6,8,64]{3,2,1,0:T(8,128)}, u32[]{:S(2)}, u32[]{:S(2)}) %collective-permute-start.1) | collective-permute-done | bytes 393248 | tf_op jit(solution)/shard_map/ppermute | solution.py:25
  228.6 1.2 broadcast_select_fusion
  229.8 1.6 copy_select_fusion.1
  231.4 14.7 %collective-permute-done = f32[32,6,8,64]{3,2,1,0:T(8,128)} collective-permute-done((f32[32,6,8,64]{3,2,1,0:T(8,128)}, f32[32,6,8,64]{3,2,1,0:T(8,128)}, u32[]{:S(2)}, u32[]{:S(2)}) %collective-permute-start) | collective-permute-done | bytes 393248 | tf_op jit(solution)/shard_map/ppermute | solution.py:25
  246.1 1.2 broadcast_select_fusion.1
  247.3 7.6 %fusion.80 = f32[32,8,8,64]{3,2,1,0:T(8,128)} fusion(f32[32,8,8,64]{3,2,1,0:T(8,128)S(1)} %reshape.17, f32[32,8,8,6]{3,2,1,0:T(8,128)S(1)} %copy-done.2, f32[32,8,8,6]{3,2,1,0:T(8,128)S(1)} %copy-done.3, f32[32,8,6,64]{3,2,1,0:T(8,128)S(1)} %copy_select_fusion, f32[32,8,6,64]{3,2,1,0:T(8,128)S(1)} %copy_select_fusion.1, ...), kind=kLoop, calls=%fused_computation.145 | loop fusion | flops 12058624 | bytes 2719744 | tf_op jit(solution)/shard_map/mul | solution.py:84
  254.9 3.3 %copy.99 = f32[32,8,8,64]{0,3,2,1:T(8,128)} copy(f32[32,8,8,64]{3,2,1,0:T(8,128)} %fusion.80) | data formatting | bytes 1048576 | tf_op jit(solution)/shard_map/mul | solution.py:84
  258.1 2.9 bitcast_add_fusion
  261.1 42.8 %scatter_fusion = f32[32,4096]{0,1:T(8,128)} fusion(f32[32,4096]{0,1:T(8,128)} %bitcast_add_fusion, s32[8192]{0:T(1024)S(1)} %fusion.88, f32[8192,32]{1,0:T(8,128)} %bitcast.34), kind=kCustom, calls=%fused_computation.1 | custom fusion | flops 262144 | bytes 3178496 | tf_op jit(solution)/shard_map/scatter-add | solution.py:117
  303.9 2.2 copy.110
  306.1 0.1 multiply_subtract_fusion
  306.3 13.8 %all_to_all.19 = f32[32,4,1024]{2,0,1:T(8,128)S(1)} all-to-all(f32[32,4,1024]{2,0,1:T(8,128)S(1)} %bitcast.35), channel_id=1, replica_groups=mesh['band'=4,'dom'=128] {'band'}, dimensions={1} | all-to-all | bytes 1048576 | tf_op jit(solution)/shard_map/all_to_all | solution.py:121
  320.1 1.8 fusion.106
  (51 shorter events, 0.3 us)
Async XLA Ops:
  0.0 320.1 %copy-start = (f32[128,128]{1,0:T(8,128)S(1)}, f32[128,128]{1,0:T(8,128)}, u32[]{:S(2)}) copy-start(f32[128,128]{1,0:T(8,128)} %param.17) | copy-start | bytes 196612
  0.0 1.7 copy-start.7
  29.4 3.6 %copy-start.5 = (f32[64,8,128]{2,1,0:T(8,128)S(1)}, f32[64,8,128]{2,1,0:T(8,128)}, u32[]{:S(2)}) copy-start(f32[64,8,128]{2,1,0:T(8,128)} %param.15) | copy-start | bytes 786436
  29.4 6.8 %copy-start.11 = (s32[64]{0:T(128)S(1)}, s32[64]{0:T(128)}, u32[]{:S(2)}) copy-start(s32[64]{0:T(128)} %param.12) | copy-start | bytes 772
  32.9 10.9 %copy-start.12 = (f32[64]{0:T(128)}, f32[64]{0:T(128)S(1)}, u32[]{:S(2)}) copy-start(f32[64]{0:T(128)S(1)} %compare_convert_fusion) | copy-start | bytes 772
  35.6 0.6 copy-start.10
  37.4 31.9 %collective-permute-start.11 = (f32[4,8,32]{2,0,1:T(4,128)S(1)}, f32[4,8,32]{2,0,1:T(4,128)S(1)}, u32[]{:S(2)}, u32[]{:S(2)}) collective-permute-start(f32[4,8,32]{2,0,1:T(4,128)S(1)} %get-tuple-element.12), channel_id=1, source_target_pairs={{1,0},{2,1},{3,2},{4,3},{5,4},{6,5},{7,6},{8,7},{9,8},{10,9},{11,1... | collective-permute-start | bytes 12296 | tf_op jit(solution)/shard_map/ppermute | solution.py:25
  41.9 38.9 %collective-permute-start.10 = (f32[4,8,32]{2,0,1:T(4,128)S(1)}, f32[4,8,32]{2,0,1:T(4,128)S(1)}, u32[]{:S(2)}, u32[]{:S(2)}) collective-permute-start(f32[4,8,32]{2,0,1:T(4,128)S(1)} %get-tuple-element.13), channel_id=1, source_target_pairs={{0,1},{1,2},{2,3},{3,4},{4,5},{5,6},{6,7},{7,8},{8,9},{9,10},{10,1... | collective-permute-start | bytes 12296 | tf_op jit(solution)/shard_map/ppermute | solution.py:25
  43.8 39.0 %collective-permute-start.9 = (f32[4,8,32]{2,0,1:T(4,128)S(1)}, f32[4,8,32]{2,0,1:T(4,128)S(1)}, u32[]{:S(2)}, u32[]{:S(2)}) collective-permute-start(f32[4,8,32]{2,0,1:T(4,128)S(1)} %get-tuple-element.14), channel_id=1, source_target_pairs={{4,0},{5,1},{6,2},{7,3},{8,4},{9,5},{10,6},{11,7},{12,8},{13,9},{1... | collective-permute-start | bytes 12296 | tf_op jit(solution)/shard_map/ppermute | solution.py:25
  50.1 39.6 %collective-permute-start.8 = (f32[4,8,32]{2,0,1:T(4,128)S(1)}, f32[4,8,32]{2,0,1:T(4,128)S(1)}, u32[]{:S(2)}, u32[]{:S(2)}) collective-permute-start(f32[4,8,32]{2,0,1:T(4,128)S(1)} %get-tuple-element.15), channel_id=1, source_target_pairs={{0,4},{1,5},{2,6},{3,7},{4,8},{5,9},{6,10},{7,11},{8,12},{9,13},{1... | collective-permute-start | bytes 12296 | tf_op jit(solution)/shard_map/ppermute | solution.py:25
  53.6 43.6 %collective-permute-start.7 = (f32[4,8,32]{2,0,1:T(4,128)S(1)}, f32[4,8,32]{2,0,1:T(4,128)S(1)}, u32[]{:S(2)}, u32[]{:S(2)}) collective-permute-start(f32[4,8,32]{2,0,1:T(4,128)S(1)} %get-tuple-element.16), channel_id=1, source_target_pairs={{16,0},{17,1},{18,2},{19,3},{20,4},{21,5},{22,6},{23,7},{24,8},{25... | collective-permute-start | bytes 12296 | tf_op jit(solution)/shard_map/ppermute | solution.py:25
  69.3 31.1 %collective-permute-start.6 = (f32[4,8,32]{2,0,1:T(4,128)S(1)}, f32[4,8,32]{2,0,1:T(4,128)}, u32[]{:S(2)}, u32[]{:S(2)}) collective-permute-start(f32[4,8,32]{2,0,1:T(4,128)S(1)} %get-tuple-element.11), channel_id=1, source_target_pairs={{0,16},{1,17},{2,18},{3,19},{4,20},{5,21},{6,22},{7,23},{8,24},{9,... | collective-permute-start | bytes 12296 | tf_op jit(solution)/shard_map/ppermute | solution.py:25
  77.4 2.4 copy-start.4
  77.4 23.8 %copy-start.9 = (f32[4,8,8]{2,1,0:T(8,128)S(1)}, f32[4,8,8]{2,1,0:T(8,128)}, u32[]{:S(2)}) copy-start(f32[4,8,8]{2,1,0:T(8,128)} %param.16) | copy-start | bytes 3076
  80.8 126.9 %collective-permute-start.5 = (f32[32,8,8,6]{0,2,3,1:T(8,128)}, f32[32,8,8,6]{0,2,3,1:T(8,128)}, u32[]{:S(2)}, u32[]{:S(2)}) collective-permute-start(f32[32,8,8,6]{0,2,3,1:T(8,128)} %copy.97), channel_id=1, source_target_pairs={{0,1},{1,2},{2,3},{3,4},{4,5},{5,6},{6,7},{7,8},{8,9},{9,10},{10,1... | collective-permute-start | bytes 147464 | tf_op jit(solution)/shard_map/ppermute | solution.py:25
  82.9 132.9 %collective-permute-start.4 = (f32[32,8,8,6]{0,2,3,1:T(8,128)}, f32[32,8,8,6]{0,2,3,1:T(8,128)}, u32[]{:S(2)}, u32[]{:S(2)}) collective-permute-start(f32[32,8,8,6]{0,2,3,1:T(8,128)} %copy.95), channel_id=1, source_target_pairs={{1,0},{2,1},{3,2},{4,3},{5,4},{6,5},{7,6},{8,7},{9,8},{10,9},{11,1... | collective-permute-start | bytes 147464 | tf_op jit(solution)/shard_map/ppermute | solution.py:25
  89.7 132.4 %collective-permute-start.3 = (f32[32,8,6,64]{3,1,2,0:T(8,128)}, f32[32,8,6,64]{3,1,2,0:T(8,128)}, u32[]{:S(2)}, u32[]{:S(2)}) collective-permute-start(f32[32,8,6,64]{3,1,2,0:T(8,128)} %copy.93), channel_id=1, source_target_pairs={{0,4},{1,5},{2,6},{3,7},{4,8},{5,9},{6,10},{7,11},{8,12},{9,13},{1... | collective-permute-start | bytes 1179656 | tf_op jit(solution)/shard_map/ppermute | solution.py:25
  97.2 132.6 %collective-permute-start.2 = (f32[32,8,6,64]{3,1,2,0:T(8,128)}, f32[32,8,6,64]{3,1,2,0:T(8,128)}, u32[]{:S(2)}, u32[]{:S(2)}) collective-permute-start(f32[32,8,6,64]{3,1,2,0:T(8,128)} %copy.91), channel_id=1, source_target_pairs={{4,0},{5,1},{6,2},{7,3},{8,4},{9,5},{10,6},{11,7},{12,8},{13,9},{1... | collective-permute-start | bytes 1179656 | tf_op jit(solution)/shard_map/ppermute | solution.py:25
  101.3 8.4 %collective-permute-start.12 = (f32[4,8,32]{2,0,1:T(4,128)S(1)}, f32[4,8,32]{2,0,1:T(4,128)S(1)}, u32[]{:S(2)}, u32[]{:S(2)}) collective-permute-start(f32[4,8,32]{2,0,1:T(4,128)S(1)} %bitcast.40), channel_id=1, source_target_pairs={{16,0},{17,1},{18,2},{19,3},{20,4},{21,5},{22,6},{23,7},{24,8},{25... | collective-permute-start | bytes 12296 | tf_op jit(solution)/shard_map/ppermute | solution.py:25
  109.7 9.4 %collective-permute-start.13 = (f32[4,8,32]{2,0,1:T(4,128)S(1)}, f32[4,8,32]{2,0,1:T(4,128)S(1)}, u32[]{:S(2)}, u32[]{:S(2)}) collective-permute-start(f32[4,8,32]{2,0,1:T(4,128)S(1)} %bitcast.41), channel_id=1, source_target_pairs={{0,16},{1,17},{2,18},{3,19},{4,20},{5,21},{6,22},{7,23},{8,24},{9,... | collective-permute-start | bytes 12296 | tf_op jit(solution)/shard_map/ppermute | solution.py:25
  119.1 50.8 %collective-permute-start.14 = (f32[4,8,32]{2,0,1:T(4,128)S(1)}, f32[4,8,32]{2,0,1:T(4,128)S(1)}, u32[]{:S(2)}, u32[]{:S(2)}) collective-permute-start(f32[4,8,32]{2,0,1:T(4,128)S(1)} %bitcast.42), channel_id=1, source_target_pairs={{4,0},{5,1},{6,2},{7,3},{8,4},{9,5},{10,6},{11,7},{12,8},{13,9},{1... | collective-permute-start | bytes 12296 | tf_op jit(solution)/shard_map/ppermute | solution.py:25
  169.9 10.4 %collective-permute-start.15 = (f32[4,8,32]{2,0,1:T(4,128)S(1)}, f32[4,8,32]{2,0,1:T(4,128)S(1)}, u32[]{:S(2)}, u32[]{:S(2)}) collective-permute-start(f32[4,8,32]{2,0,1:T(4,128)S(1)} %bitcast.43), channel_id=1, source_target_pairs={{0,4},{1,5},{2,6},{3,7},{4,8},{5,9},{6,10},{7,11},{8,12},{9,13},{1... | collective-permute-start | bytes 12296 | tf_op jit(solution)/shard_map/ppermute | solution.py:25
  180.3 5.6 %collective-permute-start.16 = (f32[4,8,32]{2,0,1:T(4,128)S(1)}, f32[4,8,32]{2,0,1:T(4,128)S(1)}, u32[]{:S(2)}, u32[]{:S(2)}) collective-permute-start(f32[4,8,32]{2,0,1:T(4,128)S(1)} %bitcast.44), channel_id=1, source_target_pairs={{1,0},{2,1},{3,2},{4,3},{5,4},{6,5},{7,6},{8,7},{9,8},{10,9},{11,1... | collective-permute-start | bytes 12296 | tf_op jit(solution)/shard_map/ppermute | solution.py:25
  185.9 7.7 %collective-permute-start.17 = (f32[4,8,32]{2,0,1:T(4,128)S(1)}, f32[4,8,32]{2,0,1:T(4,128)S(1)}, u32[]{:S(2)}, u32[]{:S(2)}) collective-permute-start(f32[4,8,32]{2,0,1:T(4,128)S(1)} %bitcast.45), channel_id=1, source_target_pairs={{0,1},{1,2},{2,3},{3,4},{4,5},{5,6},{6,7},{7,8},{8,9},{9,10},{10,1... | collective-permute-start | bytes 12296 | tf_op jit(solution)/shard_map/ppermute | solution.py:25
  193.7 34.9 %collective-permute-start.1 = (f32[32,6,8,64]{3,2,1,0:T(8,128)}, f32[32,6,8,64]{3,2,1,0:T(8,128)}, u32[]{:S(2)}, u32[]{:S(2)}) collective-permute-start(f32[32,6,8,64]{3,2,1,0:T(8,128)} %get-tuple-element.6), channel_id=1, source_target_pairs={{0,16},{1,17},{2,18},{3,19},{4,20},{5,21},{6,22},{7,23},{8,24},{9,... | collective-permute-start | bytes 1179656 | tf_op jit(solution)/shard_map/ppermute | solution.py:25
  207.8 38.3 %collective-permute-start = (f32[32,6,8,64]{3,2,1,0:T(8,128)}, f32[32,6,8,64]{3,2,1,0:T(8,128)}, u32[]{:S(2)}, u32[]{:S(2)}) collective-permute-start(f32[32,6,8,64]{3,2,1,0:T(8,128)} %get-tuple-element.5), channel_id=1, source_target_pairs={{16,0},{17,1},{18,2},{19,3},{20,4},{21,5},{22,6},{23,7},{24,8},{25... | collective-permute-start | bytes 1179656 | tf_op jit(solution)/shard_map/ppermute | solution.py:25
  229.8 17.5 %copy-start.2 = (f32[32,8,8,6]{3,2,1,0:T(8,128)S(1)}, f32[32,8,8,6]{3,2,1,0:T(8,128)}, u32[]{:S(2)}) copy-start(f32[32,8,8,6]{3,2,1,0:T(8,128)} %copy.98) | copy-start | bytes 147460
  229.8 17.5 %copy-start.3 = (f32[32,8,8,6]{3,2,1,0:T(8,128)S(1)}, f32[32,8,8,6]{3,2,1,0:T(8,128)}, u32[]{:S(2)}) copy-start(f32[32,8,8,6]{3,2,1,0:T(8,128)} %copy.96) | copy-start | bytes 147460
  254.9 3.3 %copy-start.8 = (f32[4096]{0:T(1024)S(1)}, f32[4096]{0:T(1024)}, u32[]{:S(2)}) copy-start(f32[4096]{0:T(1024)} %param.11) | copy-start | bytes 49156
  303.9 2.3 copy-start.1
  303.9 2.3 copy-start.6
where the time goes:
time: 323 us; the launch traced here: 322 us
  waiting for transfers between devices  90.4 us (28%)
  starting transfers between devices  80 us (25%)
  other arithmetic  61.2 us (19%)
  local copies, waits for them, and re-layouts  58.8 us (18%)
  matrix products  16.5 us (5%)
  blocking collectives  13.8 us (4%)
    ppermute x18, waiting for transfers between devices, shifted(): return lax.ppermute(block, axis, route)  90.4 us
    ppermute x18, starting transfers between devices, shifted(): return lax.ppermute(block, axis, route)  80 us
    scatter-add x1, other arithmetic, body(): projected = jnp.zeros_like(states).at[:, tile_cells].add(spread)  42.8 us
    gather x2, local copies, waits for them, and re-layouts, body(): picked = states[:, tile_cells]  30.5 us
    all_to_all x1, blocking collectives, body(): lax.all_to_all(filtered, 'band', split_axis=1, concat_axis=0, tiled=True)  13.8 us
    transpose x1, matrix products, body(): spread = jnp.einsum('tjp,tjs->stp', weights, tile_coef, precision=highest)  9.27 us
    slice x5, local copies, waits for them, and re-layouts, body(): lax.slice_in_dim(blockgrid, 0, radius, axis=dimension)  8.12 us
    mul x1, other arithmetic, body(): kinetic = (-0.5 * laplace).reshape(blocks, cell_count)  7.56 us
  transfers between devices with their start and end apart: 18, of which 8 were waited for; matrix products, arithmetic and copies ran while one was open for 12% of the time, Pallas kernels for 0%

commit v1 on v0

v1 whole, which is shorter than its diff:
```python
import functools

import jax
import jax.numpy as jnp
import numpy as np
from jax import lax
from jax.experimental import pallas as pl
from jax.experimental.pallas import tpu as pltpu
from jax.sharding import PartitionSpec as P

MESH = pl.DeviceIdType.MESH
F32 = jnp.float32
BF16 = jnp.bfloat16

STENCIL = (
    -5369.0 / 1800.0,
    12.0 / 7.0,
    -15.0 / 56.0,
    10.0 / 189.0,
    -1.0 / 112.0,
    2.0 / 1925.0,
    -1.0 / 16632.0,
)
W = tuple(-0.075 * w for w in STENCIL)
QUARTER = 1024
LINE = 512


def split(value):
    high = value.astype(BF16)
    return high, (value - high.astype(F32)).astype(BF16)


def split_constant(matrix):
    high = matrix.astype(jnp.bfloat16)
    low = (matrix - high.astype(np.float64)).astype(jnp.bfloat16)
    return np.asarray(high), np.asarray(low)


def z_matrices():
    lane = np.arange(256)
    gap = np.abs(lane[:, None] - lane[None, :])
    weights = np.array(W + (0.0,) * 256)
    inside = np.where((lane[:, None] // 64 == lane[None, :] // 64) & (gap > 0), weights[np.minimum(gap, 7)], 0.0)
    slot = np.arange(128)
    cell = np.arange(QUARTER)
    same = slot[:, None] // 8 == cell[None, :] // 64
    z = cell[None, :] % 64
    i = slot[:, None] % 8
    used = same & (i < 6)
    pick_high = (used & (z == 58 + i)).astype(np.float64)
    pick_low = (used & (z == i)).astype(np.float64)
    below = np.where(used, weights[np.minimum(z + 6 - i, 7)], 0.0)
    above = np.where(used, weights[np.minimum(64 + i - z, 7)], 0.0)
    pick = np.concatenate([pick_high, pick_low]).astype(jnp.bfloat16)
    return *split_constant(inside), pick, *split_constant(np.concatenate([below, above]))


def dot(a, b, ca=1, cb=0):
    return lax.dot_general(a, b, (((ca,), (cb,)), ((), ())), preferred_element_type=F32)


def kernel(
    count_ref,
    states,
    previous,
    potential,
    tile_atom,
    tile_cells,
    projectors,
    coupling,
    rotation,
    in_hi,
    in_lo,
    pick,
    face_hi,
    face_lo,
    out,
    filt,
    y_land,
    x_send,
    x_land,
    z_send,
    z_land,
    s_send,
    s_land,
    c_send,
    c_land,
    f_land,
    g_hi,
    g_lo,
    member,
    y_ss,
    y_rs,
    x_ss,
    x_rs,
    z_ss,
    z_rs,
    s_ss,
    s_rs,
    c_ss,
    c_rs,
    f_ss,
    f_rs,
):
    band = lax.axis_index("band")
    dom = lax.axis_index("dom")
    gz = lax.rem(dom, 4)
    gy = lax.rem(dom // 4, 4)
    gx = dom // 16
    steps = (16, -16, 4, -4, 1, -1)
    exists = (gx < 7, gx > 0, gy < 3, gy > 0, gz < 3, gz > 0)

    def there(direction):
        return (band, dom + steps[direction])

    def lanes(quarter):
        return pl.multiple_of(quarter * QUARTER, QUARTER)

    barrier = pltpu.get_barrier_semaphore()
    for direction in range(6):

        @pl.when(exists[direction])
        def _():
            pl.semaphore_signal(barrier, inc=1, device_id=there(direction), device_id_type=MESH)

    for other in range(1, 4):
        pl.semaphore_signal(
            barrier, inc=1, device_id=(lax.rem(band + other, 4), dom), device_id_type=MESH
        )
    partners = 3
    for direction in range(6):
        partners = partners + jnp.where(exists[direction], 1, 0)
    pl.semaphore_wait(barrier, partners)

    def y_copies(side, k):
        quarter = lax.rem(band + 1 + k, 4)
        copies = []
        for i in range(2):
            start = pl.multiple_of(lanes(quarter) + i * LINE + (128 if side == 0 else 0), 128)
            copies.append(
                pltpu.make_async_remote_copy(
                    src_ref=states.at[:, pl.ds(start, 384)],
                    dst_ref=y_land.at[side, :, pl.ds(start, 384)],
                    send_sem=y_ss.at[side, k, i],
                    recv_sem=y_rs.at[side, k, i],
                    device_id=there(2 + side),
                    device_id_type=MESH,
                )
            )
        return copies

    def y_start(k, _):
        for side in range(2):

            @pl.when(exists[2 + side])
            def _():
                for copy in y_copies(side, k):
                    copy.start()

        return 0

    lax.fori_loop(0, 4, y_start, 0)

    def x_parts(g, _):
        rows = pl.ds(pl.multiple_of(g * 8, 8), 8)
        for column in range(4):
            layer = [states[rows, pl.ds(x * LINE + column * 128, 128)] for x in range(8)]
            for target in range(6):
                total = W[6] * layer[target + 2]
                for m in range(target + 3, 8):
                    total = total + W[target + 8 - m] * layer[m]
                x_send[0, rows, pl.ds(target * LINE + column * 128, 128)] = total
            for target in range(2, 8):
                total = W[6] * layer[target - 2]
                for m in range(target - 2):
                    total = total + W[m + 8 - target] * layer[m]
                x_send[1, rows, pl.ds(target * LINE + column * 128, 128)] = total
        return 0

    lax.fori_loop(0, 4, x_parts, 0)

    def x_copy(side, k):
        quarter = lax.rem(band + 1 + k, 4)
        block = pl.ds(lanes(quarter), QUARTER)
        return pltpu.make_async_remote_copy(
            src_ref=x_send.at[side, :, block],
            dst_ref=x_land.at[side, :, block],
            send_sem=x_ss.at[side, k],
            recv_sem=x_rs.at[side, k],
            device_id=there(side),
            device_id_type=MESH,
        )

    def x_used(side, k):
        quarter = lax.rem(band + 1 + k, 4)
        return quarter < 3 if side == 0 else quarter > 0

    def x_start(k, _):
        for side in range(2):

            @pl.when(exists[side] & x_used(side, k))
            def _():
                x_copy(side, k).start()

        return 0

    lax.fori_loop(0, 4, x_start, 0)

    pieces = []
    for quarter in range(4):
        pieces.extend(split(states[:, pl.ds(quarter * QUARTER, QUARTER)]))
    picked = dot(jnp.concatenate(pieces, axis=0), pick[...], 1, 1)
    for quarter in range(4):
        both = picked[quarter * 64 : quarter * 64 + 32] + picked[quarter * 64 + 32 : quarter * 64 + 64]
        z_send[0, :, pl.ds(quarter * 128, 128)] = both[:, 0:128]
        z_send[1, :, pl.ds(quarter * 128, 128)] = both[:, 128:256]

    def z_copy(side):
        return pltpu.make_async_remote_copy(
            src_ref=z_send.at[side],
            dst_ref=z_land.at[side],
            send_sem=z_ss.at[side],
            recv_sem=z_rs.at[side],
            device_id=there(4 + side),
            device_id_type=MESH,
        )

    for side in range(2):

        @pl.when(exists[4 + side])
        def _():
            z_copy(side).start()

        @pl.when(jnp.logical_not(exists[5 - side]))
        def _():
            z_land[side] = jnp.zeros((32, 512), F32)

        @pl.when(jnp.logical_not(exists[3 - side]))
        def _():
            y_land[side] = jnp.zeros((32, 4096), F32)

    def tile_pair(pair, _):
        spread = []
        for which in range(2):
            t = pair * 2 + which
            cells = tile_cells[pl.ds(t, 1), :]
            high, low = cells >> 8, cells & 255
            w = projectors[t]
            w_hi = w.astype(BF16).astype(F32)
            w_lo = w - w_hi
            blocks_hi, blocks_lo = [], []
            for h in range(16):
                here = high == h
                blocks_hi.append(jnp.where(here, w_hi, 0.0))
                blocks_lo.append(jnp.where(here, w_lo, 0.0))
            left = jnp.concatenate(
                [jnp.concatenate(blocks_hi, 0).astype(BF16), jnp.concatenate(blocks_lo, 0).astype(BF16)], axis=1
            )
            hot = jnp.where(lax.broadcasted_iota(jnp.int32, (256, 128), 0) == low, 1.0, 0.0).astype(BF16)
            spread.append(dot(left, jnp.concatenate([hot, hot], axis=1), 1, 1))
        rows = pl.ds(pl.multiple_of(pair * 16, 16), 16)
        for h in range(16):
            both = jnp.concatenate([spread[0][h * 8 : h * 8 + 8], spread[1][h * 8 : h * 8 + 8]], axis=0)
            both_hi, both_lo = split(both)
            g_hi[rows, pl.ds(h * 256, 256)] = both_hi
            g_lo[rows, pl.ds(h * 256, 256)] = both_lo
        return 0

    lax.fori_loop(0, 32, tile_pair, 0)

    relative = (tile_atom[...] - dom * 4).astype(F32).astype(BF16)
    repeat = (
        lax.broadcasted_iota(jnp.int32, (64, 512), 0) == lax.broadcasted_iota(jnp.int32, (64, 512), 1) // 8
    )
    owner = dot(
        jnp.broadcast_to(relative.astype(F32), (16, 64)).astype(BF16), jnp.where(repeat, 1.0, 0.0).astype(BF16)
    )[0:1]
    slot = lax.broadcasted_iota(jnp.int32, (1, 512), 1)
    owner = jnp.where(slot // 8 < count_ref[0], owner, 1000.0)
    row = lax.broadcasted_iota(jnp.int32, (32, 512), 0)
    same_j = (row & 7) == (lax.broadcasted_iota(jnp.int32, (32, 512), 1) & 7)
    atom = (row // 8).astype(F32)
    for number, step in enumerate((0,) + steps):
        match = same_j & (atom + 4.0 * step == owner)
        member[pl.ds(number * 32, 32), :] = jnp.where(match, 1.0, 0.0).astype(BF16)

    st_hi, st_lo = split(states[...])
    partial_hi = dot(g_hi[...], jnp.concatenate([st_hi, st_lo], axis=0), 1, 1)
    partial_value = partial_hi[:, 0:32] + partial_hi[:, 32:64] + dot(g_lo[...], st_hi, 1, 1)
    part_hi, part_lo = split(partial_value)
    sums = dot(member[...], part_hi) + dot(member[...], part_lo)
    messages = []
    for number in range(7):
        messages.append(
            jnp.concatenate([sums[number * 32 + a * 8 : number * 32 + a * 8 + 8] for a in range(4)], axis=1)
        )
    for direction in range(6):
        s_send[direction] = messages[direction + 1]

    def s_copy(direction):
        return pltpu.make_async_remote_copy(
            src_ref=s_send.at[direction],
            dst_ref=s_land.at[direction],
            send_sem=s_ss.at[direction],
            recv_sem=s_rs.at[direction],
            device_id=there(direction),
            device_id_type=MESH,
        )

    for direction in range(6):

        @pl.when(exists[direction])
        def _():
            s_copy(direction).start()

        @pl.when(jnp.logical_not(exists[direction ^ 1]))
        def _():
            s_land[direction] = jnp.zeros((8, 128), F32)
            c_land[direction] = jnp.zeros((8, 128), F32)

    def base(g, _):
        rows = pl.ds(pl.multiple_of(g * 8, 8), 8)
        for column in range(4):
            layer = [states[rows, pl.ds(x * LINE + column * 128, 128)] for x in range(8)]
            for x in range(8):
                block = pl.ds(x * LINE + column * 128, 128)
                total = layer[x] * (3.0 * W[0] - 1.2 + 0.15 * potential[:, block]) - 0.3 * previous[rows, block]
                for k in range(1, 7):
                    pair = [layer[m] for m in (x - k, x + k) if 0 <= m < 8]
                    if pair:
                        total = total + W[k] * (pair[0] + pair[1] if len(pair) == 2 else pair[0])
                filt[rows, block] = total
        return 0

    lax.fori_loop(0, 4, base, 0)
    blocks = [states[:, pl.ds(i * 256, 256)] for i in range(16)]
    tall_hi, tall_lo = split(jnp.concatenate(blocks, axis=0))
    inside = dot(tall_hi, in_hi[...]) + dot(tall_lo, in_hi[...]) + dot(tall_hi, in_lo[...])
    for i in range(16):
        filt[:, pl.ds(i * 256, 256)] += inside[i * 32 : i * 32 + 32]

    for side in range(2):

        @pl.when(exists[5 - side])
        def _():
            z_copy(side).wait_recv()

    faces = []
    for quarter in range(4):
        block = pl.ds(quarter * 128, 128)
        faces.append(jnp.concatenate([z_land[0, :, block], z_land[1, :, block]], axis=1))
    faces_hi, faces_lo = split(jnp.concatenate(faces, axis=0))
    edge = dot(faces_hi, face_hi[...]) + dot(faces_lo, face_hi[...]) + dot(faces_hi, face_lo[...])
    for quarter in range(4):
        filt[:, pl.ds(quarter * QUARTER, QUARTER)] += edge[quarter * 32 : quarter * 32 + 32]

    owned = messages[0]
    for direction in range(6):

        @pl.when(exists[direction ^ 1])
        def _():
            s_copy(direction).wait_recv()

        owned = owned + s_land[direction]
    lane = lax.broadcasted_iota(jnp.int32, (8, 128), 1) // 32
    coef = jnp.zeros((8, 128), F32)
    for j in range(8):
        column = jnp.zeros((8, 128), F32)
        for a in range(4):
            column = jnp.where(lane == a, coupling[a][:, j : j + 1], column)
        coef = coef + column * owned[j : j + 1, :]
    c_send[...] = coef

    def c_copy(direction):
        return pltpu.make_async_remote_copy(
            src_ref=c_send,
            dst_ref=c_land.at[direction],
            send_sem=c_ss.at[direction],
            recv_sem=c_rs.at[direction],
            device_id=there(direction),
            device_id_type=MESH,
        )

    for direction in range(6):

        @pl.when(exists[direction])
        def _():
            c_copy(direction).start()

    for direction in range(6):

        @pl.when(exists[direction ^ 1])
        def _():
            c_copy(direction).wait_recv()

    known = [coef] + [c_land[direction ^ 1] for direction in range(6)]
    table = jnp.concatenate([block[:, a * 32 : a * 32 + 32] for block in known for a in range(4)], axis=0)
    table_hi, table_lo = split(table)
    tile_coef = dot(jnp.concatenate([table_hi, table_lo], axis=1).T, member[...]).astype(BF16)

    def project(i, _):
        block = pl.ds(pl.multiple_of(i * 512, 512), 512)
        both = dot(tile_coef, g_hi[:, block])
        more = dot(tile_coef[0:32], g_lo[:, block])
        filt[:, block] += 0.15 * (both[0:32] + both[32:64] + more)
        return 0

    lax.fori_loop(0, 8, project, 0)

    left_half = lax.broadcasted_iota(jnp.int32, (8, 128), 1) < 64

    def finish(quarter):
        def line(n, _):
            rows = pl.ds(pl.multiple_of(lax.rem(n, 4) * 8, 8), 8)
            start = lanes(quarter) + n // 4 * LINE

            def at(offset):
                return pl.ds(pl.multiple_of(start + offset, 128), 128)

            run = [y_land[0, rows, at(128 + 128 * i)] for i in range(3)]
            run += [states[rows, at(128 * i)] for i in range(4)]
            run += [y_land[1, rows, at(128 * i)] for i in range(3)]
            turned = [pltpu.roll(v, 64, 1) for v in run]
            odd = []
            for g in range(3, 8):
                odd.append(
                    W[1] * (turned[g] + turned[g - 1])
                    + W[3] * (turned[min(g + 1, 9)] + turned[g - 2])
                    + W[5] * (turned[min(g + 2, 9)] + turned[g - 3])
                )
            for g in range(4):
                total = filt[rows, at(128 * g)]
                for k in (2, 4, 6):
                    total = total + W[k] * (run[g + 3 + k // 2] + run[g + 3 - k // 2])
                filt[rows, at(128 * g)] = total + jnp.where(left_half, odd[g], odd[g + 1])
            return 0

        lax.fori_loop(0, 8, line, 0)

    def f_copy(k):
        quarter = lax.rem(band + 1 + k, 4)
        return pltpu.make_async_remote_copy(
            src_ref=filt.at[:, pl.ds(lanes(quarter), QUARTER)],
            dst_ref=f_land.at[k],
            send_sem=f_ss.at[k],
            recv_sem=f_rs.at[k],
            device_id=(quarter, dom),
            device_id_type=MESH,
        )

    def rotate(value, source, first):
        v_hi, v_lo = split(value)
        r_hi, r_lo = split(rotation[pl.ds(pl.multiple_of(source * 32, 32), 32), :])
        product = dot(
            jnp.concatenate([v_hi, v_lo, v_hi], axis=0), jnp.concatenate([r_hi, r_hi, r_lo], axis=0), 0, 0
        )
        if first:
            out[...] = product
        else:
            out[...] += product

    def arrived(k, first):
        f_copy(k).wait_recv()
        rotate(f_land[k], lax.rem(band + 3 - k, 4), first)

    for k in range(4):
        quarter = lax.rem(band + 1 + k, 4)
        for side in range(2):

            @pl.when(exists[side ^ 1] & x_used(side, k))
            def _():
                x_copy(side, k).wait_recv()
                block = pl.ds(lanes(quarter), QUARTER)
                filt[:, block] += x_land[side, :, block]

            @pl.when(exists[3 - side])
            def _():
                for copy in y_copies(side, k):
                    copy.wait_recv()

        finish(quarter)
        if k < 3:
            f_copy(k).start()
        if k > 0:
            arrived(k - 1, k == 1)
    rotate(filt[:, pl.ds(lanes(band), QUARTER)], band, False)

    for k in range(4):
        for side in range(2):

            @pl.when(exists[side] & x_used(side, k))
            def _():
                x_copy(side, k).wait_send()

            @pl.when(exists[2 + side])
            def _():
                for copy in y_copies(side, k):
                    copy.wait_send()

    for side in range(2):

        @pl.when(exists[4 + side])
        def _():
            z_copy(side).wait_send()

    for direction in range(6):

        @pl.when(exists[direction])
        def _():
            s_copy(direction).wait_send()
            c_copy(direction).wait_send()

    for k in range(3):
        f_copy(k).wait_send()


def body(states, previous, potential, tile_atom, tile_cells, tile_count, projectors, coupling, rotation):
    vmem = pl.BlockSpec(memory_space=pltpu.VMEM)
    dma = pltpu.SemaphoreType.DMA
    return pl.pallas_call(
        kernel,
        out_shape=jax.ShapeDtypeStruct((QUARTER, 128), F32),
        in_specs=[pl.BlockSpec(memory_space=pltpu.SMEM)] + [vmem] * 13,
        out_specs=vmem,
        scratch_shapes=[
            pltpu.VMEM((32, 4096), F32),
            pltpu.VMEM((2, 32, 4096), F32),
            pltpu.VMEM((2, 32, 4096), F32),
            pltpu.VMEM((2, 32, 4096), F32),
            pltpu.VMEM((2, 32, 512), F32),
            pltpu.VMEM((2, 32, 512), F32),
            pltpu.VMEM((6, 8, 128), F32),
            pltpu.VMEM((6, 8, 128), F32),
            pltpu.VMEM((8, 128), F32),
            pltpu.VMEM((6, 8, 128), F32),
            pltpu.VMEM((3, 32, QUARTER), F32),
            pltpu.VMEM((512, 4096), BF16),
            pltpu.VMEM((512, 4096), BF16),
            pltpu.VMEM((224, 512), BF16),
            dma((2, 4, 2)),
            dma((2, 4, 2)),
            dma((2, 4)),
            dma((2, 4)),
            dma((2,)),
            dma((2,)),
            dma((6,)),
            dma((6,)),
            dma((6,)),
            dma((6,)),
            dma((3,)),
            dma((3,)),
        ],
        compiler_params=pltpu.CompilerParams(
            collective_id=0, has_side_effects=True, vmem_limit_bytes=48 * 1024 * 1024
        ),
        name="chebyshev_step",
    )(
        tile_count,
        states,
        previous,
        potential.reshape(1, -1),
        tile_atom.reshape(1, -1),
        tile_cells,
        projectors,
        coupling,
        rotation,
        *(jnp.asarray(m) for m in z_matrices()),
    )


def solution(mesh):
    placed = (
        P("band", "dom"),
        P("band", "dom"),
        P("dom"),
        P("dom"),
        P("dom", None),
        P("dom"),
        P("dom", None, None),
        P("dom", None, None),
        P(),
    )
    return jax.shard_map(
        body, mesh=mesh, in_specs=placed, out_specs=P(("dom", "band"), None), check_vma=False
    )
```

time: 323 us -> 82.8 us (0.26)
  the two profiles are of different devices: /device:TPU:66 before, /device:TPU:11 now
where the time goes in v1:
time: 82.8 us; the launch traced here: 82.2 us
  Pallas kernels  69.1 us (83%)
  local copies, waits for them, and re-layouts  12.4 us (15%)
    pallas_call x1, Pallas kernels, body(): pl.pallas_call(kernel, out_shape=jax.ShapeDtypeStruct((QUARTER, 128), F32...  69.1 us
    unnamed x27, local copies, waits for them, and re-layouts  12.4 us

profile of v1, /device:TPU:11, one launch (start us, length us, event | category | flops | bytes accessed | tf_op | source)
XLA Modules:
  0.0 82.2 jit_solution(14905980001565089461)
XLA Ops:
  0.7 0.0 copy-start.12
  0.7 0.6 copy-done.12
  1.3 0.0 copy-start
  1.3 1.0 %copy-done = f32[32,4096]{1,0:T(8,128)S(1)} copy-done((f32[32,4096]{1,0:T(8,128)S(1)}, f32[32,4096]{1,0:T(8,128)}, u32[]{:S(2)}) %copy-start) | copy-done | bytes 524312
  2.4 0.0 copy-start.1
  2.4 1.0 %copy-done.1 = f32[32,4096]{1,0:T(8,128)S(1)} copy-done((f32[32,4096]{1,0:T(8,128)S(1)}, f32[32,4096]{1,0:T(8,128)}, u32[]{:S(2)}) %copy-start.1) | copy-done | bytes 524312
  3.4 0.0 copy-start.2
  3.4 1.0 %copy-done.2 = bf16[256,1024]{1,0:T(8,128)(2,1)S(1)} copy-done((bf16[256,1024]{1,0:T(8,128)(2,1)S(1)}, bf16[256,1024]{1,0:T(8,128)(2,1)}, u32[]{:S(2)}) %copy-start.2) | copy-done | bytes 524312
  4.4 0.0 copy-start.3
  4.4 1.0 %copy-done.3 = bf16[256,1024]{1,0:T(8,128)(2,1)S(1)} copy-done((bf16[256,1024]{1,0:T(8,128)(2,1)S(1)}, bf16[256,1024]{1,0:T(8,128)(2,1)}, u32[]{:S(2)}) %copy-start.3) | copy-done | bytes 524312
  5.5 0.0 copy-start.4
  5.5 1.0 %copy-done.4 = bf16[256,1024]{1,0:T(8,128)(2,1)S(1)} copy-done((bf16[256,1024]{1,0:T(8,128)(2,1)S(1)}, bf16[256,1024]{1,0:T(8,128)(2,1)}, u32[]{:S(2)}) %copy-start.4) | copy-done | bytes 524312
  6.5 0.0 copy-start.5
  6.5 0.9 %copy-done.5 = f32[64,8,128]{2,1,0:T(8,128)S(1)} copy-done((f32[64,8,128]{2,1,0:T(8,128)S(1)}, f32[64,8,128]{2,1,0:T(8,128)}, u32[]{:S(2)}) %copy-start.5) | copy-done | bytes 262168
  7.5 0.0 copy-start.6
  7.5 0.9 %copy-done.6 = bf16[256,256]{1,0:T(8,128)(2,1)S(1)} copy-done((bf16[256,256]{1,0:T(8,128)(2,1)S(1)}, bf16[256,256]{1,0:T(8,128)(2,1)}, u32[]{:S(2)}) %copy-start.6) | copy-done | bytes 131096
  8.4 0.0 copy-start.7
  8.4 0.9 %copy-done.7 = bf16[256,256]{1,0:T(8,128)(2,1)S(1)} copy-done((bf16[256,256]{1,0:T(8,128)(2,1)S(1)}, bf16[256,256]{1,0:T(8,128)(2,1)}, u32[]{:S(2)}) %copy-start.7) | copy-done | bytes 131096
  9.3 0.0 copy-start.8
  9.3 0.8 %copy-done.8 = f32[128,128]{1,0:T(8,128)S(1)} copy-done((f32[128,128]{1,0:T(8,128)S(1)}, f32[128,128]{1,0:T(8,128)}, u32[]{:S(2)}) %copy-start.8) | copy-done | bytes 65560
  10.1 0.0 copy-start.9
  10.1 0.8 copy-done.9
  10.9 0.0 copy-start.10
  10.9 0.7 copy-done.10
  11.6 0.0 copy-start.11
  11.6 0.7 copy-done.11
  12.3 69.1 %chebyshev_step.1 = f32[1024,128]{1,0:T(8,128)S(1)} custom-call(s32[1]{0:T(128)S(6)} %copy.16.count_ref, f32[32,4096]{1,0:T(8,128)S(1)} %copy-done, f32[32,4096]{1,0:T(8,128)S(1)} %copy-done.1, f32[1,4096]{1,0:T(1,128)S(1)} %bitcast.2, s32[1,64]{1,0:T(1,128)S(1)} %bitcast.3, s32[64,128]{1,0:T(8,128)S(1)} %copy-done.9, f32[64,8,128]{2,1,0:T(8,128)S(1)} %copy-done.5, ...), custom_call_target="tpu_custom_call" | custom-call | tf_op jit(solution)/shard_map/chebyshev_step/pallas_call | solution.py:521
  81.4 0.8 copy.17
Async XLA Ops:
  0.7 0.7 copy-start.12
  1.3 1.0 %copy-start = (f32[32,4096]{1,0:T(8,128)S(1)}, f32[32,4096]{1,0:T(8,128)}, u32[]{:S(2)}) copy-start(f32[32,4096]{1,0:T(8,128)} %states.1) | copy-start | bytes 1572868
  2.4 1.0 %copy-start.1 = (f32[32,4096]{1,0:T(8,128)S(1)}, f32[32,4096]{1,0:T(8,128)}, u32[]{:S(2)}) copy-start(f32[32,4096]{1,0:T(8,128)} %previous.1) | copy-start | bytes 1572868
  3.4 1.0 %copy-start.2 = (bf16[256,1024]{1,0:T(8,128)(2,1)S(1)}, bf16[256,1024]{1,0:T(8,128)(2,1)}, u32[]{:S(2)}) copy-start(bf16[256,1024]{1,0:T(8,128)(2,1)} %constant.14.clone.face_lo) | copy-start | bytes 1572868
  4.4 1.0 %copy-start.3 = (bf16[256,1024]{1,0:T(8,128)(2,1)S(1)}, bf16[256,1024]{1,0:T(8,128)(2,1)}, u32[]{:S(2)}) copy-start(bf16[256,1024]{1,0:T(8,128)(2,1)} %constant.13.clone.face_hi) | copy-start | bytes 1572868
  5.5 1.0 %copy-start.4 = (bf16[256,1024]{1,0:T(8,128)(2,1)S(1)}, bf16[256,1024]{1,0:T(8,128)(2,1)}, u32[]{:S(2)}) copy-start(bf16[256,1024]{1,0:T(8,128)(2,1)} %constant.12.clone.pick) | copy-start | bytes 1572868
  6.5 0.9 %copy-start.5 = (f32[64,8,128]{2,1,0:T(8,128)S(1)}, f32[64,8,128]{2,1,0:T(8,128)}, u32[]{:S(2)}) copy-start(f32[64,8,128]{2,1,0:T(8,128)} %projectors.1) | copy-start | bytes 786436
  7.5 0.9 %copy-start.6 = (bf16[256,256]{1,0:T(8,128)(2,1)S(1)}, bf16[256,256]{1,0:T(8,128)(2,1)}, u32[]{:S(2)}) copy-start(bf16[256,256]{1,0:T(8,128)(2,1)} %constant.11.clone.in_lo) | copy-start | bytes 393220
  8.4 0.9 %copy-start.7 = (bf16[256,256]{1,0:T(8,128)(2,1)S(1)}, bf16[256,256]{1,0:T(8,128)(2,1)}, u32[]{:S(2)}) copy-start(bf16[256,256]{1,0:T(8,128)(2,1)} %constant.10.clone.in_hi) | copy-start | bytes 393220
  9.3 0.8 %copy-start.8 = (f32[128,128]{1,0:T(8,128)S(1)}, f32[128,128]{1,0:T(8,128)}, u32[]{:S(2)}) copy-start(f32[128,128]{1,0:T(8,128)} %rotation.1) | copy-start | bytes 196612
  10.1 0.8 copy-start.9
  10.9 0.7 copy-start.10
  11.6 0.7 copy-start.11

commit v2 on v1

v2 whole, which is shorter than its diff:
```python
import jax
import jax.numpy as jnp
from jax import lax
from jax.experimental import pallas as pl
from jax.experimental.pallas import tpu as pltpu
from jax.sharding import PartitionSpec as P

MESH = pl.DeviceIdType.MESH
F32 = jnp.float32
BF16 = jnp.bfloat16

STENCIL = (
    -5369.0 / 1800.0,
    12.0 / 7.0,
    -15.0 / 56.0,
    10.0 / 189.0,
    -1.0 / 112.0,
    2.0 / 1925.0,
    -1.0 / 16632.0,
)
W = tuple(-0.075 * w for w in STENCIL)
QUARTER = 1024
LINE = 512


def split(value):
    high = value.astype(BF16)
    return high, (value - high.astype(F32)).astype(BF16)


def faces_of(rows, columns):
    row = lax.broadcasted_iota(jnp.int32, (rows, 1), 0)
    column = lax.broadcasted_iota(jnp.int32, (rows, columns), 1)
    side, line, i = row // 128, (row // 8 & 15) * 64, row & 7
    used = i < 6
    cell = jnp.where(used, line + jnp.where(side == 0, 58 + i, i), -1)
    pick = jnp.where(column == cell, 1.0, 0.0).astype(BF16)
    face = jnp.zeros((rows, columns), F32)
    for n in range(1, 7):
        z = jnp.where(side == 0, n - 6 + i, 64 + i - n)
        place = jnp.where(used & (z >= 0) & (z < 64), line + z, -1)
        face = jnp.where(column == place, W[n], face)
    return pick, *split(face)


def inside_of(size):
    row = lax.broadcasted_iota(jnp.int32, (size, size), 0)
    column = lax.broadcasted_iota(jnp.int32, (size, size), 1)
    gap = jnp.where(row // 64 == column // 64, jnp.abs(row - column), 0)
    weight = jnp.zeros((size, size), F32)
    for n in range(1, 7):
        weight = jnp.where(gap == n, W[n], weight)
    return split(weight)


def dot(a, b, ca=1, cb=0):
    return lax.dot_general(a, b, (((ca,), (cb,)), ((), ())), preferred_element_type=F32)


def kernel(
    count_ref,
    states_in,
    previous_in,
    potential_in,
    atom_in,
    cells_in,
    projectors_in,
    coupling_in,
    rotation_in,
    out,
    states,
    previous,
    potential,
    tile_atom,
    tile_cells,
    projectors,
    coupling,
    rotation,
    load_sem,
    face_hi,
    face_lo,
    filt,
    y_land,
    x_send,
    x_land,
    z_send,
    z_land,
    s_send,
    s_land,
    c_send,
    c_land,
    f_land,
    g_hi,
    g_lo,
    member,
    y_ss,
    y_rs,
    x_ss,
    x_rs,
    z_ss,
    z_rs,
    s_ss,
    s_rs,
    c_ss,
    c_rs,
    f_ss,
    f_rs,
):
    band = lax.axis_index("band")
    dom = lax.axis_index("dom")
    gz = lax.rem(dom, 4)
    gy = lax.rem(dom // 4, 4)
    gx = dom // 16
    steps = (16, -16, 4, -4, 1, -1)
    exists = (gx < 7, gx > 0, gy < 3, gy > 0, gz < 3, gz > 0)

    loads = [
        pltpu.make_async_copy(source, target, load_sem.at[n])
        for n, (source, target) in enumerate(
            (
                (states_in, states),
                (cells_in, tile_cells),
                (projectors_in, projectors),
                (atom_in, tile_atom),
                (previous_in, previous),
                (potential_in, potential),
                (coupling_in, coupling),
                (rotation_in, rotation),
            )
        )
    ]
    for load in loads:
        load.start()

    def there(direction):
        return (band, dom + steps[direction])

    def quarter_of(k):
        return lax.rem(band + 1 + k, 4)

    def lanes(quarter):
        return pl.multiple_of(quarter * QUARTER, QUARTER)

    def remote(source, target, sent, landed, device):
        return pltpu.make_async_remote_copy(
            src_ref=source,
            dst_ref=target,
            send_sem=sent,
            recv_sem=landed,
            device_id=device,
            device_id_type=MESH,
        )

    def start(needed, copies):
        @pl.when(needed)
        def _():
            for copy in copies():
                copy.start()

    def landed(needed, copies):
        @pl.when(needed)
        def _():
            for copy in copies():
                copy.wait_recv()

    def sent(needed, copies):
        @pl.when(needed)
        def _():
            for copy in copies():
                copy.wait_send()

    outer = (gy == 0) | (gy == 3)
    inner = jnp.logical_not(outer)
    even = lax.rem(gy, 2) == 0
    partner = (band, jnp.where(even, dom + 4, dom - 4))
    far = (band, jnp.where(gy < 2, dom + 8, dom - 8))
    partner_side = jnp.where(even, 1, 0)
    six = jnp.where(gy == 0, 128, 0)

    barrier = pltpu.get_barrier_semaphore()
    for direction in range(6):

        @pl.when(exists[direction])
        def _():
            pl.semaphore_signal(barrier, inc=1, device_id=there(direction), device_id_type=MESH)

    for other in range(1, 4):
        pl.semaphore_signal(
            barrier, inc=1, device_id=(lax.rem(band + other, 4), dom), device_id_type=MESH
        )
    pl.semaphore_signal(barrier, inc=1, device_id=far, device_id_type=MESH)
    partners = 4
    for direction in range(6):
        partners = partners + jnp.where(exists[direction], 1, 0)
    pl.semaphore_wait(barrier, partners)

    def y_all(k):
        block = pl.ds(lanes(quarter_of(k)), QUARTER)
        return [
            remote(states_in.at[:, block], y_land.at[1 - partner_side, :, block], y_ss.at[0, k], y_rs.at[0, k], partner)
        ]

    def y_six(source, number, k, device):
        copies = []
        for i in range(2):
            block = pl.ds(pl.multiple_of(lanes(quarter_of(k)) + i * LINE + six, 128), 384)
            copies.append(
                remote(
                    source.at[:, block],
                    y_land.at[1 - partner_side, :, block],
                    y_ss.at[number + i, k],
                    y_rs.at[number + i, k],
                    device,
                )
            )
        return copies

    def y_outer(k):
        return y_six(states_in, 1, k, partner)

    def y_relay(k):
        return y_six(y_land.at[partner_side], 3, k, far)

    def y_start(k):
        start(inner, lambda: y_all(k))
        start(outer, lambda: y_outer(k))

    def hand_on(k):
        landed(outer, lambda: y_all(k))
        start(outer, lambda: y_relay(k))

    def x_copy(side, k):
        block = pl.ds(lanes(quarter_of(k)), QUARTER)
        return [
            remote(
                x_send.at[side, :, block], x_land.at[side, :, block], x_ss.at[side, k], x_rs.at[side, k], there(side)
            )
        ]

    def x_used(side, k):
        return quarter_of(k) < 3 if side == 0 else quarter_of(k) > 0

    def x_start(k):
        for side in range(2):
            start(exists[side] & x_used(side, k), lambda: x_copy(side, k))

    def z_copy(side):
        return [remote(z_send.at[side], z_land.at[side], z_ss.at[side], z_rs.at[side], there(4 + side))]

    def s_copy(direction):
        return [
            remote(
                s_send.at[direction], s_land.at[direction], s_ss.at[direction], s_rs.at[direction], there(direction)
            )
        ]

    def c_copy(direction):
        return [remote(c_send, c_land.at[direction], c_ss.at[direction], c_rs.at[direction], there(direction))]

    def f_copy(k):
        return [
            remote(
                filt.at[:, pl.ds(lanes(quarter_of(k)), QUARTER)],
                f_land.at[k],
                f_ss.at[k],
                f_rs.at[k],
                (quarter_of(k), dom),
            )
        ]

    y_start(0)

    def x_parts(g, _):
        rows = pl.ds(pl.multiple_of(g * 8, 8), 8)
        for column in range(4):
            layer = [states[rows, pl.ds(x * LINE + column * 128, 128)] for x in range(8)]
            for target in range(6):
                total = W[6] * layer[target + 2]
                for m in range(target + 3, 8):
                    total = total + W[target + 8 - m] * layer[m]
                x_send[0, rows, pl.ds(target * LINE + column * 128, 128)] = total
            for target in range(2, 8):
                total = W[6] * layer[target - 2]
                for m in range(target - 2):
                    total = total + W[m + 8 - target] * layer[m]
                x_send[1, rows, pl.ds(target * LINE + column * 128, 128)] = total
        return 0

    loads[0].wait()
    lax.fori_loop(0, 4, x_parts, 0)
    x_start(0)

    pick, *face = faces_of(256, QUARTER)
    face_hi[...], face_lo[...] = face
    pieces = []
    for quarter in range(4):
        pieces.extend(split(states[:, pl.ds(quarter * QUARTER, QUARTER)]))
    picked = dot(jnp.concatenate(pieces, axis=0), pick, 1, 1)
    for quarter in range(4):
        both = picked[quarter * 64 : quarter * 64 + 32] + picked[quarter * 64 + 32 : quarter * 64 + 64]
        z_send[0, :, pl.ds(quarter * 128, 128)] = both[:, 0:128]
        z_send[1, :, pl.ds(quarter * 128, 128)] = both[:, 128:256]

    for side in range(2):
        start(exists[4 + side], lambda: z_copy(side))

        @pl.when(jnp.logical_not(exists[5 - side]))
        def _():
            z_land[side] = jnp.zeros((32, 512), F32)

        @pl.when(jnp.logical_not(exists[3 - side]))
        def _():
            y_land[side] = jnp.zeros((32, 4096), F32)

    for direction in range(6):

        @pl.when(jnp.logical_not(exists[direction ^ 1]))
        def _():
            s_land[direction] = jnp.zeros((8, 128), F32)
            c_land[direction] = jnp.zeros((8, 128), F32)

    loads[1].wait()
    loads[2].wait()

    def tile_pair(pair, _):
        spread = []
        for which in range(2):
            t = pair * 2 + which
            cells = tile_cells[pl.ds(t, 1), :]
            high, low = cells >> 8, cells & 255
            w = projectors[t]
            w_hi = w.astype(BF16).astype(F32)
            w_lo = w - w_hi
            blocks_hi, blocks_lo = [], []
            for h in range(16):
                here = high == h
                blocks_hi.append(jnp.where(here, w_hi, 0.0))
                blocks_lo.append(jnp.where(here, w_lo, 0.0))
            left = jnp.concatenate(
                [jnp.concatenate(blocks_hi, 0).astype(BF16), jnp.concatenate(blocks_lo, 0).astype(BF16)], axis=1
            )
            hot = jnp.where(lax.broadcasted_iota(jnp.int32, (256, 128), 0) == low, 1.0, 0.0).astype(BF16)
            spread.append(dot(left, jnp.concatenate([hot, hot], axis=1), 1, 1))
        rows = pl.ds(pl.multiple_of(pair * 16, 16), 16)
        for h in range(16):
            both = jnp.concatenate([spread[0][h * 8 : h * 8 + 8], spread[1][h * 8 : h * 8 + 8]], axis=0)
            both_hi, both_lo = split(both)
            g_hi[rows, pl.ds(h * 256, 256)] = both_hi
            g_lo[rows, pl.ds(h * 256, 256)] = both_lo
        return 0

    lax.fori_loop(0, 32, tile_pair, 0)

    loads[3].wait()
    relative = (tile_atom[...] - dom * 4).astype(F32).astype(BF16)
    repeat = (
        lax.broadcasted_iota(jnp.int32, (64, 512), 0) == lax.broadcasted_iota(jnp.int32, (64, 512), 1) // 8
    )
    owner = dot(
        jnp.broadcast_to(relative.astype(F32), (16, 64)).astype(BF16), jnp.where(repeat, 1.0, 0.0).astype(BF16)
    )[0:1]
    slot = lax.broadcasted_iota(jnp.int32, (1, 512), 1)
    owner = jnp.where(slot // 8 < count_ref[0], owner, 1000.0)
    row = lax.broadcasted_iota(jnp.int32, (32, 512), 0)
    same_j = (row & 7) == (lax.broadcasted_iota(jnp.int32, (32, 512), 1) & 7)
    atom = (row // 8).astype(F32)
    for number, step in enumerate((0,) + steps):
        match = same_j & (atom + 4.0 * step == owner)
        member[pl.ds(number * 32, 32), :] = jnp.where(match, 1.0, 0.0).astype(BF16)

    st_hi, st_lo = split(states[...])
    partial_hi = dot(g_hi[...], jnp.concatenate([st_hi, st_lo], axis=0), 1, 1)
    partial_value = partial_hi[:, 0:32] + partial_hi[:, 32:64] + dot(g_lo[...], st_hi, 1, 1)
    part_hi, part_lo = split(partial_value)
    sums = dot(member[...], part_hi) + dot(member[...], part_lo)
    messages = []
    for number in range(7):
        messages.append(
            jnp.concatenate([sums[number * 32 + a * 8 : number * 32 + a * 8 + 8] for a in range(4)], axis=1)
        )
    for direction in range(6):
        s_send[direction] = messages[direction + 1]
    for direction in range(6):
        start(exists[direction], lambda: s_copy(direction))
    y_start(1)
    x_start(1)

    def base(g, _):
        rows = pl.ds(pl.multiple_of(g * 8, 8), 8)
        for column in range(4):
            layer = [states[rows, pl.ds(x * LINE + column * 128, 128)] for x in range(8)]
            for x in range(8):
                block = pl.ds(x * LINE + column * 128, 128)
                total = layer[x] * (3.0 * W[0] - 1.2 + 0.15 * potential[:, block]) - 0.3 * previous[rows, block]
                for k in range(1, 7):
                    pair = [layer[m] for m in (x - k, x + k) if 0 <= m < 8]
                    if pair:
                        total = total + W[k] * (pair[0] + pair[1] if len(pair) == 2 else pair[0])
                filt[rows, block] = total
        return 0

    for n in (4, 5):
        loads[n].wait()
    lax.fori_loop(0, 4, base, 0)
    blocks = [states[:, pl.ds(i * 256, 256)] for i in range(16)]
    tall_hi, tall_lo = split(jnp.concatenate(blocks, axis=0))
    in_hi, in_lo = inside_of(256)
    inside = dot(tall_hi, in_hi) + dot(tall_lo, in_hi) + dot(tall_hi, in_lo)
    for i in range(16):
        filt[:, pl.ds(i * 256, 256)] += inside[i * 32 : i * 32 + 32]

    hand_on(0)

    for side in range(2):
        landed(exists[5 - side], lambda: z_copy(side))
    faces = []
    for quarter in range(4):
        block = pl.ds(quarter * 128, 128)
        faces.append(jnp.concatenate([z_land[0, :, block], z_land[1, :, block]], axis=1))
    faces_hi, faces_lo = split(jnp.concatenate(faces, axis=0))
    edge = dot(faces_hi, face_hi[...]) + dot(faces_lo, face_hi[...]) + dot(faces_hi, face_lo[...])
    for quarter in range(4):
        filt[:, pl.ds(quarter * QUARTER, QUARTER)] += edge[quarter * 32 : quarter * 32 + 32]

    loads[6].wait()
    loads[7].wait()
    lane = lax.broadcasted_iota(jnp.int32, (8, 128), 1) // 32
    mixing = []
    for j in range(8):
        column = jnp.zeros((8, 128), F32)
        for a in range(4):
            column = jnp.where(lane == a, coupling[a][:, j : j + 1], column)
        mixing.append(column)
    owned = messages[0]
    for direction in range(6):
        landed(exists[direction ^ 1], lambda: s_copy(direction))
        owned = owned + s_land[direction]
    coef = mixing[0] * owned[0:1, :]
    for j in range(1, 8):
        coef = coef + mixing[j] * owned[j : j + 1, :]
    c_send[...] = coef
    for direction in range(6):
        start(exists[direction], lambda: c_copy(direction))
    for k in (2, 3):
        y_start(k)
        x_start(k)

    hand_on(1)

    for direction in range(6):
        landed(exists[direction ^ 1], lambda: c_copy(direction))
    known = [coef] + [c_land[direction ^ 1] for direction in range(6)]
    table = jnp.concatenate([block[:, a * 32 : a * 32 + 32] for block in known for a in range(4)], axis=0)
    table_hi, table_lo = split(table)
    tile_coef = dot(jnp.concatenate([table_hi, table_lo], axis=1).T, member[...]).astype(BF16)

    def project(i, _):
        block = pl.ds(pl.multiple_of(i * 512, 512), 512)
        both = dot(tile_coef, g_hi[:, block])
        more = dot(tile_coef[0:32], g_lo[:, block])
        filt[:, block] += 0.15 * (both[0:32] + both[32:64] + more)
        return 0

    lax.fori_loop(0, 8, project, 0)

    left_half = lax.broadcasted_iota(jnp.int32, (8, 128), 1) < 64

    def finish(k):
        quarter = quarter_of(k)
        for side in range(2):

            @pl.when(exists[side ^ 1] & x_used(side, k))
            def _():
                x_copy(side, k)[0].wait_recv()
                block = pl.ds(lanes(quarter), QUARTER)
                filt[:, block] += x_land[side, :, block]

        landed(inner, lambda: y_outer(k))
        landed(inner, lambda: y_relay(k))

        def line(n, _):
            rows = pl.ds(pl.multiple_of(lax.rem(n, 4) * 8, 8), 8)
            begin = lanes(quarter) + n // 4 * LINE

            def at(offset):
                return pl.ds(pl.multiple_of(begin + offset, 128), 128)

            run = [y_land[0, rows, at(128 + 128 * i)] for i in range(3)]
            run += [states[rows, at(128 * i)] for i in range(4)]
            run += [y_land[1, rows, at(128 * i)] for i in range(3)]
            turned = [pltpu.roll(v, 64, 1) for v in run]
            odd = []
            for g in range(3, 8):
                odd.append(
                    W[1] * (turned[g] + turned[g - 1])
                    + W[3] * (turned[min(g + 1, 9)] + turned[g - 2])
                    + W[5] * (turned[min(g + 2, 9)] + turned[g - 3])
                )
            for g in range(4):
                total = filt[rows, at(128 * g)]
                for n_far in (2, 4, 6):
                    total = total + W[n_far] * (run[g + 3 + n_far // 2] + run[g + 3 - n_far // 2])
                filt[rows, at(128 * g)] = total + jnp.where(left_half, odd[g], odd[g + 1])
            return 0

        lax.fori_loop(0, 8, line, 0)

    def rotate(value, source, first):
        v_hi, v_lo = split(value)
        r_hi, r_lo = split(rotation[pl.ds(pl.multiple_of(source * 32, 32), 32), :])
        product = dot(
            jnp.concatenate([v_hi, v_lo, v_hi], axis=0), jnp.concatenate([r_hi, r_hi, r_lo], axis=0), 0, 0
        )
        if first:
            out[...] = product
        else:
            out[...] += product

    always = band >= 0

    def arrived(k):
        landed(always, lambda: f_copy(k))
        rotate(f_land[k], lax.rem(band + 3 - k, 4), k == 0)

    finish(0)
    start(always, lambda: f_copy(0))
    hand_on(2)
    finish(1)
    start(always, lambda: f_copy(1))
    finish(2)
    start(always, lambda: f_copy(2))
    hand_on(3)
    for k in range(3):
        arrived(k)
    finish(3)
    rotate(filt[:, pl.ds(lanes(band), QUARTER)], band, False)

    for k in range(4):
        sent(inner, lambda: y_all(k))
        sent(outer, lambda: y_outer(k))
        sent(outer, lambda: y_relay(k))
        for side in range(2):
            sent(exists[side] & x_used(side, k), lambda: x_copy(side, k))
    for side in range(2):
        sent(exists[4 + side], lambda: z_copy(side))
    for direction in range(6):
        sent(exists[direction], lambda: s_copy(direction))
        sent(exists[direction], lambda: c_copy(direction))
    for k in range(3):
        sent(always, lambda: f_copy(k))


def body(states, previous, potential, tile_atom, tile_cells, tile_count, projectors, coupling, rotation):
    vmem = pl.BlockSpec(memory_space=pltpu.VMEM)
    dma = pltpu.SemaphoreType.DMA
    operands = (
        states,
        previous,
        potential.reshape(1, -1),
        tile_atom.reshape(1, -1),
        tile_cells,
        projectors,
        coupling,
        rotation,
    )
    return pl.pallas_call(
        kernel,
        out_shape=jax.ShapeDtypeStruct((QUARTER, 128), F32),
        in_specs=[pl.BlockSpec(memory_space=pltpu.SMEM)] + [pl.BlockSpec(memory_space=pltpu.HBM)] * 8,
        out_specs=vmem,
        scratch_shapes=[
            *(pltpu.VMEM(operand.shape, operand.dtype) for operand in operands),
            dma((8,)),
            pltpu.VMEM((256, QUARTER), BF16),
            pltpu.VMEM((256, QUARTER), BF16),
            pltpu.VMEM((32, 4096), F32),
            pltpu.VMEM((2, 32, 4096), F32),
            pltpu.VMEM((2, 32, 4096), F32),
            pltpu.VMEM((2, 32, 4096), F32),
            pltpu.VMEM((2, 32, 512), F32),
            pltpu.VMEM((2, 32, 512), F32),
            pltpu.VMEM((6, 8, 128), F32),
            pltpu.VMEM((6, 8, 128), F32),
            pltpu.VMEM((8, 128), F32),
            pltpu.VMEM((6, 8, 128), F32),
            pltpu.VMEM((3, 32, QUARTER), F32),
            pltpu.VMEM((512, 4096), BF16),
            pltpu.VMEM((512, 4096), BF16),
            pltpu.VMEM((224, 512), BF16),
            dma((5, 4)),
            dma((5, 4)),
            dma((2, 4)),
            dma((2, 4)),
            dma((2,)),
            dma((2,)),
            dma((6,)),
            dma((6,)),
            dma((6,)),
            dma((6,)),
            dma((3,)),
            dma((3,)),
        ],
        compiler_params=pltpu.CompilerParams(
            collective_id=0, has_side_effects=True, vmem_limit_bytes=64 * 1024 * 1024
        ),
        name="chebyshev_step",
    )(tile_count, *operands)


def solution(mesh):
    placed = (
        P("band", "dom"),
        P("band", "dom"),
        P("dom"),
        P("dom"),
        P("dom", None),
        P("dom"),
        P("dom", None, None),
        P("dom", None, None),
        P(),
    )
    return jax.shard_map(
        body, mesh=mesh, in_specs=placed, out_specs=P(("dom", "band"), None), check_vma=False
    )
```

time: 82.8 us -> 59.2 us (0.71)
  the two profiles are of different devices: /device:TPU:11 before, /device:TPU:67 now
where the time goes in v2:
time: 59.2 us; the launch traced here: 59 us
  Pallas kernels  56.4 us (95%)
  local copies, waits for them, and re-layouts  1.87 us (3%)
  between operations  0.66 us (1%)
    pallas_call x1, Pallas kernels, body(): pl.pallas_call(kernel, out_shape=jax.ShapeDtypeStruct((QUARTER, 128), F32...  56.4 us
    unnamed x1, local copies, waits for them, and re-layouts  1.87 us

profile of v2, /device:TPU:67, one launch (start us, length us, event | category | flops | bytes accessed | tf_op | source)
XLA Modules:
  0.0 59.0 jit_solution(11391699358413797012)
XLA Ops:
  0.7 56.4 %chebyshev_step.1 = f32[1024,128]{1,0:T(8,128)} custom-call(s32[1]{0:T(128)S(6)} %copy.11.count_ref, f32[32,4096]{1,0:T(8,128)} %states_in.1, f32[32,4096]{1,0:T(8,128)} %previous_in.1, f32[1,4096]{1,0:T(1,128)} %bitcast.2, s32[1,64]{1,0:T(1,128)} %bitcast.3, s32[64,128]{1,0:T(8,128)} %cells_in.1, f32[64,8,128]{2,1,0:T(8,128)} %projectors_in.1, ...), custom_call_target="tpu_custom_call" | custom-call | tf_op jit(solution)/shard_map/chebyshev_step/pallas_call | solution.py:566
  57.1 1.9 %copy.12 = f32[1024,128]{1,0:T(8,128)} copy(f32[1024,128]{1,0:T(8,128)} %chebyshev_step.1) | data formatting | bytes 1048576

commit v3 on v2

--- a/solution.py
+++ b/solution.py
@@ -90,6 +90,10 @@
     c_send,
     c_land,
     f_land,
+    t_send,
+    t_land,
+    turned_rotation,
+    total_t,
     g_hi,
     g_lo,
     member,
@@ -105,6 +109,8 @@
     c_rs,
     f_ss,
     f_rs,
+    t_ss,
+    t_rs,
 ):
     band = lax.axis_index("band")
     dom = lax.axis_index("dom")
@@ -268,6 +274,11 @@
             )
         ]
 
+    def t_copy(i):
+        return [remote(t_send, t_land.at[i], t_ss.at[i], t_rs.at[i], (lax.rem(band + 1 + i, 4), dom))]
+
+    always = band >= 0
+
     y_start(0)
 
     def x_parts(g, _):
@@ -322,24 +333,33 @@
     loads[1].wait()
     loads[2].wait()
 
+    low_row = lax.broadcasted_iota(jnp.int32, (256, 128), 0).astype(F32).astype(BF16)
+    high_row = (lax.broadcasted_iota(jnp.int32, (16, 128), 0) // 8).astype(F32).astype(BF16)
+    high_rows = [high_row + jnp.asarray(2 * h, BF16) for h in range(8)]
+    zero, one = jnp.asarray(0, BF16), jnp.asarray(1, BF16)
+
     def tile_pair(pair, _):
         spread = []
         for which in range(2):
             t = pair * 2 + which
             cells = tile_cells[pl.ds(t, 1), :]
-            high, low = cells >> 8, cells & 255
+            high = jnp.broadcast_to((cells >> 8).astype(F32), (16, 128)).astype(BF16)
+            low = jnp.broadcast_to((cells & 255).astype(F32), (16, 128)).astype(BF16)
+            low = jnp.concatenate([low] * 16, axis=0)
             w = projectors[t]
             w_hi = w.astype(BF16).astype(F32)
             w_lo = w - w_hi
-            blocks_hi, blocks_lo = [], []
-            for h in range(16):
-                here = high == h
-                blocks_hi.append(jnp.where(here, w_hi, 0.0))
-                blocks_lo.append(jnp.where(here, w_lo, 0.0))
+            w_hi = jnp.concatenate([w_hi, w_hi], axis=0).astype(BF16)
+            w_lo = jnp.concatenate([w_lo, w_lo], axis=0).astype(BF16)
+            here = [high == row for row in high_rows]
             left = jnp.concatenate(
-                [jnp.concatenate(blocks_hi, 0).astype(BF16), jnp.concatenate(blocks_lo, 0).astype(BF16)], axis=1
+                [
+                    jnp.concatenate([jnp.where(mask, w_hi, zero) for mask in here], axis=0),
+                    jnp.concatenate([jnp.where(mask, w_lo, zero) for mask in here], axis=0),
+                ],
+                axis=1,
             )
-            hot = jnp.where(lax.broadcasted_iota(jnp.int32, (256, 128), 0) == low, 1.0, 0.0).astype(BF16)
+            hot = jnp.where(low_row == low, one, zero)
             spread.append(dot(left, jnp.concatenate([hot, hot], axis=1), 1, 1))
         rows = pl.ds(pl.multiple_of(pair * 16, 16), 16)
         for h in range(16):
@@ -349,7 +369,7 @@
             g_lo[rows, pl.ds(h * 256, 256)] = both_lo
         return 0
 
-    lax.fori_loop(0, 32, tile_pair, 0)
+    lax.fori_loop(0, 32, tile_pair, 0, unroll=4)
 
     loads[3].wait()
     relative = (tile_atom[...] - dom * 4).astype(F32).astype(BF16)
@@ -409,6 +429,15 @@
     for i in range(16):
         filt[:, pl.ds(i * 256, 256)] += inside[i * 32 : i * 32 + 32]
 
+    loads[7].wait()
+    order = [rotation[pl.ds(pl.multiple_of(lax.rem(band + i, 4) * 32, 32), 32), :] for i in range(4)]
+    order = jnp.concatenate(order, axis=0)
+    order_hi, order_lo = split(order)
+    across_hi, across_lo = split(order.T)
+    for i in range(4):
+        part = slice(i * 32, i * 32 + 32)
+        turned_rotation[i] = jnp.concatenate([across_hi[:, part], across_hi[:, part], across_lo[:, part]], axis=1)
+
     hand_on(0)
 
     for side in range(2):
@@ -423,7 +452,6 @@
         filt[:, pl.ds(quarter * QUARTER, QUARTER)] += edge[quarter * 32 : quarter * 32 + 32]
 
     loads[6].wait()
-    loads[7].wait()
     lane = lax.broadcasted_iota(jnp.int32, (8, 128), 1) // 32
     mixing = []
     for j in range(8):
@@ -439,29 +467,11 @@
     for j in range(1, 8):
         coef = coef + mixing[j] * owned[j : j + 1, :]
     c_send[...] = coef
+    t_send[:, 0:128] = coef
     for direction in range(6):
         start(exists[direction], lambda: c_copy(direction))
-    for k in (2, 3):
-        y_start(k)
-        x_start(k)
-
-    hand_on(1)
-
-    for direction in range(6):
-        landed(exists[direction ^ 1], lambda: c_copy(direction))
-    known = [coef] + [c_land[direction ^ 1] for direction in range(6)]
-    table = jnp.concatenate([block[:, a * 32 : a * 32 + 32] for block in known for a in range(4)], axis=0)
-    table_hi, table_lo = split(table)
-    tile_coef = dot(jnp.concatenate([table_hi, table_lo], axis=1).T, member[...]).astype(BF16)
-
-    def project(i, _):
-        block = pl.ds(pl.multiple_of(i * 512, 512), 512)
-        both = dot(tile_coef, g_hi[:, block])
-        more = dot(tile_coef[0:32], g_lo[:, block])
-        filt[:, block] += 0.15 * (both[0:32] + both[32:64] + more)
-        return 0
-
-    lax.fori_loop(0, 8, project, 0)
+    y_start(2)
+    x_start(2)
 
     left_half = lax.broadcasted_iota(jnp.int32, (8, 128), 1) < 64
 
@@ -503,37 +513,54 @@
                 filt[rows, at(128 * g)] = total + jnp.where(left_half, odd[g], odd[g + 1])
             return 0
 
-        lax.fori_loop(0, 8, line, 0)
-
-    def rotate(value, source, first):
-        v_hi, v_lo = split(value)
-        r_hi, r_lo = split(rotation[pl.ds(pl.multiple_of(source * 32, 32), 32), :])
-        product = dot(
-            jnp.concatenate([v_hi, v_lo, v_hi], axis=0), jnp.concatenate([r_hi, r_hi, r_lo], axis=0), 0, 0
-        )
-        if first:
-            out[...] = product
-        else:
-            out[...] += product
-
-    always = band >= 0
+        lax.fori_loop(0, 8, line, 0, unroll=8)
+
+    def rotated(value, i):
+        high, low = split(value)
+        return dot(turned_rotation[i], jnp.concatenate([high, low, high], axis=0))
 
     def arrived(k):
         landed(always, lambda: f_copy(k))
-        rotate(f_land[k], lax.rem(band + 3 - k, 4), k == 0)
+        total_t[...] += rotated(f_land[k], 3 - k)
 
     finish(0)
     start(always, lambda: f_copy(0))
-    hand_on(2)
+    hand_on(1)
+
+    for direction in range(6):
+        landed(exists[direction ^ 1], lambda: c_copy(direction))
+    for direction in range(6):
+        t_send[:, pl.ds((direction + 1) * 128, 128)] = c_land[direction ^ 1]
+    for i in range(3):
+        start(always, lambda: t_copy(i))
+    y_start(3)
+    x_start(3)
     finish(1)
     start(always, lambda: f_copy(1))
+    hand_on(2)
+
+    tables = [t_send]
+    for i in range(3):
+        landed(always, lambda: t_copy(i))
+    tables += [t_land.at[2 - i] for i in range(3)]
+    known = []
+    for group in range(28):
+        known.append(jnp.concatenate([table[:, group * 32 : group * 32 + 32] for table in tables], axis=1))
+    known_hi, known_lo = split(jnp.concatenate(known, axis=0))
+    mixed = 0.15 * (dot(known_hi, order_hi) + dot(known_lo, order_hi) + dot(known_hi, order_lo))
+    of_tile = dot(jnp.concatenate(split(mixed.T), axis=0), member[...]).astype(BF16)
+    mine = pl.ds(lanes(band), QUARTER)
+    nonlocal_t = dot(of_tile, g_hi[:, mine])
+    total_t[...] = nonlocal_t[0:128] + nonlocal_t[128:256] + dot(of_tile[0:128], g_lo[:, mine])
+
+    arrived(0)
     finish(2)
     start(always, lambda: f_copy(2))
+    arrived(1)
     hand_on(3)
-    for k in range(3):
-        arrived(k)
+    arrived(2)
     finish(3)
-    rotate(filt[:, pl.ds(lanes(band), QUARTER)], band, False)
+    out[...] = (total_t[...] + rotated(filt[:, mine], 0)).T
 
     for k in range(4):
         sent(inner, lambda: y_all(k))
@@ -548,6 +575,7 @@
         sent(exists[direction], lambda: c_copy(direction))
     for k in range(3):
         sent(always, lambda: f_copy(k))
+        sent(always, lambda: t_copy(k))
 
 
 def body(states, previous, potential, tile_atom, tile_cells, tile_count, projectors, coupling, rotation):
@@ -584,6 +612,10 @@
             pltpu.VMEM((8, 128), F32),
             pltpu.VMEM((6, 8, 128), F32),
             pltpu.VMEM((3, 32, QUARTER), F32),
+            pltpu.VMEM((8, 896), F32),
+            pltpu.VMEM((3, 8, 896), F32),
+            pltpu.VMEM((4, 128, 96), BF16),
+            pltpu.VMEM((128, QUARTER), F32),
             pltpu.VMEM((512, 4096), BF16),
             pltpu.VMEM((512, 4096), BF16),
             pltpu.VMEM((224, 512), BF16),
@@ -599,6 +631,8 @@
             dma((6,)),
             dma((3,)),
             dma((3,)),
+            dma((3,)),
+            dma((3,)),
         ],
         compiler_params=pltpu.CompilerParams(
             collective_id=0, has_side_effects=True, vmem_limit_bytes=64 * 1024 * 1024

time: 59.2 us -> 51.9 us (0.88)
  the two profiles are of different devices: /device:TPU:67 before, /device:TPU:7 now
where the time goes in v3:
time: 51.9 us; the launch traced here: 51.7 us
  Pallas kernels  49.2 us (95%)
  local copies, waits for them, and re-layouts  1.87 us (4%)
  between operations  0.66 us (1%)
    pallas_call x1, Pallas kernels, body(): pl.pallas_call(kernel, out_shape=jax.ShapeDtypeStruct((QUARTER, 128), F32...  49.2 us
    unnamed x1, local copies, waits for them, and re-layouts  1.87 us

profile of v3, /device:TPU:7, one launch (start us, length us, event | category | flops | bytes accessed | tf_op | source)
XLA Modules:
  0.0 51.7 jit_solution(4403366103233732190)
XLA Ops:
  0.7 49.2 %chebyshev_step.1 = f32[1024,128]{1,0:T(8,128)} custom-call(s32[1]{0:T(128)S(6)} %copy.11.count_ref, f32[32,4096]{1,0:T(8,128)} %states_in.1, f32[32,4096]{1,0:T(8,128)} %previous_in.1, f32[1,4096]{1,0:T(1,128)} %bitcast.2, s32[1,64]{1,0:T(1,128)} %bitcast.3, s32[64,128]{1,0:T(8,128)} %cells_in.1, f32[64,8,128]{2,1,0:T(8,128)} %projectors_in.1, ...), custom_call_target="tpu_custom_call" | custom-call | tf_op jit(solution)/shard_map/chebyshev_step/pallas_call | solution.py:594
  49.8 1.9 %copy.12 = f32[1024,128]{1,0:T(8,128)} copy(f32[1024,128]{1,0:T(8,128)} %chebyshev_step.1) | data formatting | bytes 1048576

commit v4 on v3

--- a/solution.py
+++ b/solution.py
@@ -81,6 +81,7 @@
     face_lo,
     filt,
     y_land,
+    aside,
     x_send,
     x_land,
     z_send,
@@ -111,6 +112,7 @@
     f_rs,
     t_ss,
     t_rs,
+    ready,
 ):
     band = lax.axis_index("band")
     dom = lax.axis_index("dom")
@@ -138,6 +140,8 @@
     for load in loads:
         load.start()
 
+    always = band >= 0
+
     def there(direction):
         return (band, dom + steps[direction])
 
@@ -181,12 +185,15 @@
     partner = (band, jnp.where(even, dom + 4, dom - 4))
     far = (band, jnp.where(gy < 2, dom + 8, dom - 8))
     partner_side = jnp.where(even, 1, 0)
-    six = jnp.where(gy == 0, 128, 0)
-
+    near_six = jnp.where(even, 128, 0)
+    far_six = 128 - near_six
+
+    later = (exists[0] & (gx != 3), exists[1] & (gx == 4))
+    earlier = (exists[0] & (gx == 3), exists[1] & (gx != 4))
     barrier = pltpu.get_barrier_semaphore()
     for direction in range(6):
 
-        @pl.when(exists[direction])
+        @pl.when(later[direction] if direction < 2 else exists[direction])
         def _():
             pl.semaphore_signal(barrier, inc=1, device_id=there(direction), device_id_type=MESH)
 
@@ -197,58 +204,109 @@
     pl.semaphore_signal(barrier, inc=1, device_id=far, device_id_type=MESH)
     partners = 4
     for direction in range(6):
-        partners = partners + jnp.where(exists[direction], 1, 0)
+        partners = partners + jnp.where(earlier[direction] if direction < 2 else exists[direction], 1, 0)
     pl.semaphore_wait(barrier, partners)
-
-    def y_all(k):
-        block = pl.ds(lanes(quarter_of(k)), QUARTER)
+    for side in range(2):
+
+        @pl.when(earlier[side])
+        def _():
+            pl.semaphore_signal(ready.at[1 - side], inc=1, device_id=there(side), device_id_type=MESH)
+
+    def later_ready():
+        for side in range(2):
+
+            @pl.when(later[side])
+            def _():
+                pl.semaphore_wait(ready.at[side], 1)
+
+    def half(m):
+        return pl.ds(m % 2 * 16, 16)
+
+    def y_all(m):
+        block = pl.ds(lanes(quarter_of(m // 2)), QUARTER)
         return [
-            remote(states_in.at[:, block], y_land.at[1 - partner_side, :, block], y_ss.at[0, k], y_rs.at[0, k], partner)
+            remote(
+                states_in.at[half(m), block],
+                y_land.at[1 - partner_side, half(m), block],
+                y_ss.at[0, m],
+                y_rs.at[0, m],
+                partner,
+            )
         ]
 
-    def y_six(source, number, k, device):
+    def y_six(m, source, source_start, target, target_start, six, number, device):
         copies = []
         for i in range(2):
-            block = pl.ds(pl.multiple_of(lanes(quarter_of(k)) + i * LINE + six, 128), 384)
+            here = pl.ds(pl.multiple_of(source_start + i * LINE + six, 128), 384)
+            over_there = pl.ds(pl.multiple_of(target_start + i * LINE + six, 128), 384)
             copies.append(
                 remote(
-                    source.at[:, block],
-                    y_land.at[1 - partner_side, :, block],
-                    y_ss.at[number + i, k],
-                    y_rs.at[number + i, k],
+                    source.at[half(m), here],
+                    target.at[half(m), over_there],
+                    y_ss.at[number + i, m],
+                    y_rs.at[number + i, m],
                     device,
                 )
             )
         return copies
 
-    def y_outer(k):
-        return y_six(states_in, 1, k, partner)
-
-    def y_relay(k):
-        return y_six(y_land.at[partner_side], 3, k, far)
-
-    def y_start(k):
-        start(inner, lambda: y_all(k))
-        start(outer, lambda: y_outer(k))
+    def y_near(m):
+        begin = lanes(quarter_of(m // 2))
+        return y_six(m, states_in, begin, y_land.at[1 - partner_side], begin, near_six, 1, partner)
+
+    def y_relay(m):
+        begin = lanes(quarter_of(m // 2))
+        return y_six(m, y_land.at[partner_side], begin, y_land.at[1 - partner_side], begin, near_six, 3, far)
+
+    def y_aside(m):
+        return y_six(m, states_in, lanes(quarter_of(3)), aside, 0, far_six, 5, far)
+
+    def y_back(m):
+        return y_six(m, aside, 0, y_land.at[partner_side], lanes(quarter_of(3)), far_six, 3, partner)
+
+    def y_start(m):
+        if m < 6:
+            start(inner, lambda: y_all(m))
+            start(outer, lambda: y_near(m))
+        else:
+            start(always, lambda: y_near(m))
 
     def hand_on(k):
-        landed(outer, lambda: y_all(k))
-        start(outer, lambda: y_relay(k))
-
-    def x_copy(side, k):
-        block = pl.ds(lanes(quarter_of(k)), QUARTER)
+        for m in (2 * k, 2 * k + 1):
+            if k < 3:
+                landed(outer, lambda: y_all(m))
+                start(outer, lambda: y_relay(m))
+            else:
+                landed(outer, lambda: y_aside(m))
+                start(outer, lambda: y_back(m))
+
+    def y_landed(k):
+        for m in (2 * k, 2 * k + 1):
+            if k < 3:
+                landed(inner, lambda: y_near(m))
+                landed(inner, lambda: y_relay(m))
+            else:
+                landed(always, lambda: y_near(m))
+                landed(inner, lambda: y_back(m))
+
+    def x_copy(side, m):
+        block = pl.ds(lanes(quarter_of(m // 2)), QUARTER)
         return [
             remote(
-                x_send.at[side, :, block], x_land.at[side, :, block], x_ss.at[side, k], x_rs.at[side, k], there(side)
+                x_send.at[side, half(m), block],
+                x_land.at[side, half(m), block],
+                x_ss.at[side, m],
+                x_rs.at[side, m],
+                there(side),
             )
         ]
 
     def x_used(side, k):
         return quarter_of(k) < 3 if side == 0 else quarter_of(k) > 0
 
-    def x_start(k):
+    def x_start(m, to=exists):
         for side in range(2):
-            start(exists[side] & x_used(side, k), lambda: x_copy(side, k))
+            start(to[side] & x_used(side, m // 2), lambda: x_copy(side, m))
 
     def z_copy(side):
         return [remote(z_send.at[side], z_land.at[side], z_ss.at[side], z_rs.at[side], there(4 + side))]
@@ -277,9 +335,11 @@
     def t_copy(i):
         return [remote(t_send, t_land.at[i], t_ss.at[i], t_rs.at[i], (lax.rem(band + 1 + i, 4), dom))]
 
-    always = band >= 0
-
     y_start(0)
+    y_start(1)
+    y_start(2)
+    for m in (6, 7):
+        start(inner, lambda: y_aside(m))
 
     def x_parts(g, _):
         rows = pl.ds(pl.multiple_of(g * 8, 8), 8)
@@ -299,7 +359,9 @@
 
     loads[0].wait()
     lax.fori_loop(0, 4, x_parts, 0)
-    x_start(0)
+    x_start(0, earlier)
+    x_start(1, earlier)
+    x_start(2, earlier)
 
     pick, *face = faces_of(256, QUARTER)
     face_hi[...], face_lo[...] = face
@@ -369,7 +431,12 @@
             g_lo[rows, pl.ds(h * 256, 256)] = both_lo
         return 0
 
-    lax.fori_loop(0, 32, tile_pair, 0, unroll=4)
+    lax.fori_loop(0, 16, tile_pair, 0, unroll=4)
+    later_ready()
+    x_start(0, later)
+    x_start(1, later)
+    x_start(2, later)
+    lax.fori_loop(16, 32, tile_pair, 0, unroll=4)
 
     loads[3].wait()
     relative = (tile_atom[...] - dom * 4).astype(F32).astype(BF16)
@@ -402,8 +469,11 @@
         s_send[direction] = messages[direction + 1]
     for direction in range(6):
         start(exists[direction], lambda: s_copy(direction))
-    y_start(1)
-    x_start(1)
+    y_start(3)
+    y_start(4)
+    x_start(3)
+    x_start(4)
+    hand_on(3)
 
     def base(g, _):
         rows = pl.ds(pl.multiple_of(g * 8, 8), 8)
@@ -470,8 +540,10 @@
     t_send[:, 0:128] = coef
     for direction in range(6):
         start(exists[direction], lambda: c_copy(direction))
-    y_start(2)
-    x_start(2)
+    y_start(5)
+    y_start(6)
+    x_start(5)
+    x_start(6)
 
     left_half = lax.broadcasted_iota(jnp.int32, (8, 128), 1) < 64
 
@@ -481,12 +553,12 @@
 
             @pl.when(exists[side ^ 1] & x_used(side, k))
             def _():
-                x_copy(side, k)[0].wait_recv()
+                for m in (2 * k, 2 * k + 1):
+                    x_copy(side, m)[0].wait_recv()
                 block = pl.ds(lanes(quarter), QUARTER)
                 filt[:, block] += x_land[side, :, block]
 
-        landed(inner, lambda: y_outer(k))
-        landed(inner, lambda: y_relay(k))
+        y_landed(k)
 
         def line(n, _):
             rows = pl.ds(pl.multiple_of(lax.rem(n, 4) * 8, 8), 8)
@@ -533,11 +605,14 @@
         t_send[:, pl.ds((direction + 1) * 128, 128)] = c_land[direction ^ 1]
     for i in range(3):
         start(always, lambda: t_copy(i))
-    y_start(3)
-    x_start(3)
+    y_start(7)
+    x_start(7)
     finish(1)
     start(always, lambda: f_copy(1))
     hand_on(2)
+
+    finish(2)
+    start(always, lambda: f_copy(2))
 
     tables = [t_send]
     for i in range(3):
@@ -554,20 +629,22 @@
     total_t[...] = nonlocal_t[0:128] + nonlocal_t[128:256] + dot(of_tile[0:128], g_lo[:, mine])
 
     arrived(0)
-    finish(2)
-    start(always, lambda: f_copy(2))
     arrived(1)
-    hand_on(3)
+    finish(3)
     arrived(2)
-    finish(3)
     out[...] = (total_t[...] + rotated(filt[:, mine], 0)).T
 
-    for k in range(4):
-        sent(inner, lambda: y_all(k))
-        sent(outer, lambda: y_outer(k))
-        sent(outer, lambda: y_relay(k))
+    for m in range(8):
+        if m < 6:
+            sent(inner, lambda: y_all(m))
+            sent(outer, lambda: y_near(m))
+            sent(outer, lambda: y_relay(m))
+        else:
+            sent(always, lambda: y_near(m))
+            sent(inner, lambda: y_aside(m))
+            sent(outer, lambda: y_back(m))
         for side in range(2):
-            sent(exists[side] & x_used(side, k), lambda: x_copy(side, k))
+            sent(exists[side] & x_used(side, m // 2), lambda: x_copy(side, m))
     for side in range(2):
         sent(exists[4 + side], lambda: z_copy(side))
     for direction in range(6):
@@ -603,6 +680,7 @@
             pltpu.VMEM((256, QUARTER), BF16),
             pltpu.VMEM((32, 4096), F32),
             pltpu.VMEM((2, 32, 4096), F32),
+            pltpu.VMEM((32, QUARTER), F32),
             pltpu.VMEM((2, 32, 4096), F32),
             pltpu.VMEM((2, 32, 4096), F32),
             pltpu.VMEM((2, 32, 512), F32),
@@ -619,10 +697,10 @@
             pltpu.VMEM((512, 4096), BF16),
             pltpu.VMEM((512, 4096), BF16),
             pltpu.VMEM((224, 512), BF16),
-            dma((5, 4)),
-            dma((5, 4)),
-            dma((2, 4)),
-            dma((2, 4)),
+            dma((7, 8)),
+            dma((7, 8)),
+            dma((2, 8)),
+            dma((2, 8)),
             dma((2,)),
             dma((2,)),
             dma((6,)),
@@ -633,6 +711,7 @@
             dma((3,)),
             dma((3,)),
             dma((3,)),
+            pltpu.SemaphoreType.REGULAR((2,)),
         ],
         compiler_params=pltpu.CompilerParams(
             collective_id=0, has_side_effects=True, vmem_limit_bytes=64 * 1024 * 1024

time: 51.9 us -> 49.9 us (0.961)
  the two profiles are of different devices: /device:TPU:7 before, /device:TPU:59 now
where the time goes in v4:
time: 49.9 us; the launch traced here: 49.7 us
  Pallas kernels  47.2 us (95%)
  local copies, waits for them, and re-layouts  1.87 us (4%)
  between operations  0.66 us (1%)
    pallas_call x1, Pallas kernels, body(): pl.pallas_call(kernel, out_shape=jax.ShapeDtypeStruct((QUARTER, 128), F32...  47.2 us
    unnamed x1, local copies, waits for them, and re-layouts  1.87 us

profile of v4, /device:TPU:59, one launch (start us, length us, event | category | flops | bytes accessed | tf_op | source)
XLA Modules:
  0.0 49.7 jit_solution(16456850310926313598)
XLA Ops:
  0.7 47.2 %chebyshev_step.1 = f32[1024,128]{1,0:T(8,128)} custom-call(s32[1]{0:T(128)S(6)} %copy.11.count_ref, f32[32,4096]{1,0:T(8,128)} %states_in.1, f32[32,4096]{1,0:T(8,128)} %previous_in.1, f32[1,4096]{1,0:T(1,128)} %bitcast.2, s32[1,64]{1,0:T(1,128)} %bitcast.3, s32[64,128]{1,0:T(8,128)} %cells_in.1, f32[64,8,128]{2,1,0:T(8,128)} %projectors_in.1, ...), custom_call_target="tpu_custom_call" | custom-call | tf_op jit(solution)/shard_map/chebyshev_step/pallas_call | solution.py:671
  47.8 1.9 %copy.12 = f32[1024,128]{1,0:T(8,128)} copy(f32[1024,128]{1,0:T(8,128)} %chebyshev_step.1) | data formatting | bytes 1048576

commit v5 on v4

--- a/solution.py
+++ b/solution.py
@@ -146,7 +146,7 @@
         return (band, dom + steps[direction])
 
     def quarter_of(k):
-        return lax.rem(band + 1 + k, 4)
+        return (lax.rem(band + 2, 4), 3 - band, band + 1 - 2 * lax.rem(band, 2), band)[k]
 
     def lanes(quarter):
         return pl.multiple_of(quarter * QUARTER, QUARTER)
@@ -333,7 +333,7 @@
         ]
 
     def t_copy(i):
-        return [remote(t_send, t_land.at[i], t_ss.at[i], t_rs.at[i], (lax.rem(band + 1 + i, 4), dom))]
+        return [remote(t_send, t_land.at[i], t_ss.at[i], t_rs.at[i], (quarter_of(i), dom))]
 
     y_start(0)
     y_start(1)
@@ -431,12 +431,12 @@
             g_lo[rows, pl.ds(h * 256, 256)] = both_lo
         return 0
 
-    lax.fori_loop(0, 16, tile_pair, 0, unroll=4)
+    lax.fori_loop(0, 16, tile_pair, 0, unroll=8)
     later_ready()
     x_start(0, later)
     x_start(1, later)
     x_start(2, later)
-    lax.fori_loop(16, 32, tile_pair, 0, unroll=4)
+    lax.fori_loop(16, 32, tile_pair, 0, unroll=8)
 
     loads[3].wait()
     relative = (tile_atom[...] - dom * 4).astype(F32).astype(BF16)
@@ -500,7 +500,7 @@
         filt[:, pl.ds(i * 256, 256)] += inside[i * 32 : i * 32 + 32]
 
     loads[7].wait()
-    order = [rotation[pl.ds(pl.multiple_of(lax.rem(band + i, 4) * 32, 32), 32), :] for i in range(4)]
+    order = [rotation[pl.ds(pl.multiple_of(source * 32, 32), 32), :] for source in (band, *map(quarter_of, range(3)))]
     order = jnp.concatenate(order, axis=0)
     order_hi, order_lo = split(order)
     across_hi, across_lo = split(order.T)
@@ -593,7 +593,7 @@
 
     def arrived(k):
         landed(always, lambda: f_copy(k))
-        total_t[...] += rotated(f_land[k], 3 - k)
+        total_t[...] += rotated(f_land[k], k + 1)
 
     finish(0)
     start(always, lambda: f_copy(0))
@@ -607,9 +607,9 @@
         start(always, lambda: t_copy(i))
     y_start(7)
     x_start(7)
+    hand_on(2)
     finish(1)
     start(always, lambda: f_copy(1))
-    hand_on(2)
 
     finish(2)
     start(always, lambda: f_copy(2))
@@ -617,7 +617,7 @@
     tables = [t_send]
     for i in range(3):
         landed(always, lambda: t_copy(i))
-    tables += [t_land.at[2 - i] for i in range(3)]
+    tables += [t_land.at[i] for i in range(3)]
     known = []
     for group in range(28):
         known.append(jnp.concatenate([table[:, group * 32 : group * 32 + 32] for table in tables], axis=1))

time: 49.9 us -> 48.8 us (0.978)
  the two profiles are of different devices: /device:TPU:59 before, /device:TPU:2 now
where the time goes in v5:
time: 48.8 us; the launch traced here: 48.6 us
  Pallas kernels  46 us (94%)
  local copies, waits for them, and re-layouts  1.87 us (4%)
  between operations  0.66 us (1%)
    pallas_call x1, Pallas kernels, body(): pl.pallas_call(kernel, out_shape=jax.ShapeDtypeStruct((QUARTER, 128), F32...  46 us
    unnamed x1, local copies, waits for them, and re-layouts  1.87 us

profile of v5, /device:TPU:2, one launch (start us, length us, event | category | flops | bytes accessed | tf_op | source)
XLA Modules:
  0.0 48.6 jit_solution(13058702404781130439)
XLA Ops:
  0.7 46.0 %chebyshev_step.1 = f32[1024,128]{1,0:T(8,128)} custom-call(s32[1]{0:T(128)S(6)} %copy.11.count_ref, f32[32,4096]{1,0:T(8,128)} %states_in.1, f32[32,4096]{1,0:T(8,128)} %previous_in.1, f32[1,4096]{1,0:T(1,128)} %bitcast.2, s32[1,64]{1,0:T(1,128)} %bitcast.3, s32[64,128]{1,0:T(8,128)} %cells_in.1, f32[64,8,128]{2,1,0:T(8,128)} %projectors_in.1, ...), custom_call_target="tpu_custom_call" | custom-call | tf_op jit(solution)/shard_map/chebyshev_step/pallas_call | solution.py:671
  46.7 1.9 %copy.12 = f32[1024,128]{1,0:T(8,128)} copy(f32[1024,128]{1,0:T(8,128)} %chebyshev_step.1) | data formatting | bytes 1048576

commit v6 on v5

--- a/solution.py
+++ b/solution.py
@@ -542,6 +542,7 @@
         start(exists[direction], lambda: c_copy(direction))
     y_start(5)
     y_start(6)
+    y_start(7)
     x_start(5)
     x_start(6)
 
@@ -605,7 +606,6 @@
         t_send[:, pl.ds((direction + 1) * 128, 128)] = c_land[direction ^ 1]
     for i in range(3):
         start(always, lambda: t_copy(i))
-    y_start(7)
     x_start(7)
     hand_on(2)
     finish(1)

time: 48.8 us -> 48.8 us (level)
  no operation moved by 1% of the time
where the time goes in v6:
time: 48.8 us; the launch traced here: 48.6 us
  Pallas kernels  46.1 us (94%)
  local copies, waits for them, and re-layouts  1.87 us (4%)
  between operations  0.66 us (1%)
    pallas_call x1, Pallas kernels, body(): pl.pallas_call(kernel, out_shape=jax.ShapeDtypeStruct((QUARTER, 128), F32...  46.1 us
    unnamed x1, local copies, waits for them, and re-layouts  1.87 us

profile of v6, /device:TPU:2, one launch (start us, length us, event | category | flops | bytes accessed | tf_op | source)
XLA Modules:
  0.0 48.6 jit_solution(8252701428833258078)
XLA Ops:
  0.7 46.1 %chebyshev_step.1 = f32[1024,128]{1,0:T(8,128)} custom-call(s32[1]{0:T(128)S(6)} %copy.11.count_ref, f32[32,4096]{1,0:T(8,128)} %states_in.1, f32[32,4096]{1,0:T(8,128)} %previous_in.1, f32[1,4096]{1,0:T(1,128)} %bitcast.2, s32[1,64]{1,0:T(1,128)} %bitcast.3, s32[64,128]{1,0:T(8,128)} %cells_in.1, f32[64,8,128]{2,1,0:T(8,128)} %projectors_in.1, ...), custom_call_target="tpu_custom_call" | custom-call | tf_op jit(solution)/shard_map/chebyshev_step/pallas_call | solution.py:671
  46.7 1.9 %copy.12 = f32[1024,128]{1,0:T(8,128)} copy(f32[1024,128]{1,0:T(8,128)} %chebyshev_step.1) | data formatting | bytes 1048576
